TPU v7x, 32 devices: a whole 2x2x4 slice. The times are simulated.
32 devices in a mesh: dp: 4 (over y, core), head: 2 (over x), blk: 4 (over z).
Axes of the slice: x: 2, y: 2, z: 4, core: 2. Of those that a mesh axis runs over, the one named last changes fastest.
Arguments:
- queries: bfloat16 [4, 1024, 8192], P('dp', ('blk', 'head')), may hold values from -6 to 6
- keys: bfloat16 [4, 1024, 1024], P('dp', ('blk', 'head')), may hold values from -6 to 6
- values: bfloat16 [4, 1024, 1024], P('dp', ('blk', 'head')), may hold values from -6 to 6
- attention_output: bfloat16 [4, 1024, 8192], P('dp', ('blk', 'head')), may hold values from -6 to 6
- output_gradient: bfloat16 [4, 1024, 8192], P('dp', ('blk', 'head')), may hold values from -6 to 6
- saved_log_normaliser: float32 [4, 64, 1024], P('dp', 'head', 'blk')
- proj_grad: bfloat16 [4, 1024, 4096], P('dp', ('blk', 'head')), may hold values from -0.125 to 0.125
- doc_lengths: int32 [4, 8], P('dp'), may hold values from 1 to 256, as said below
Outputs:
- d_queries: bfloat16 [4, 1024, 8192], P('dp', ('blk', 'head'))
- d_keys: bfloat16 [4, 1024, 1024], P('dp', ('blk', 'head'))
- d_values: bfloat16 [4, 1024, 1024], P('dp', ('blk', 'head'))
- d_wo: bfloat16 [8192, 4096], P('head', ('dp', 'blk'))
Inputs may be any that keep to these rules, and one draw needn't show every extreme that they name: `doc_lengths`: the 8 lengths of a row sum to 1024; every row holds exactly one document of 256 tokens.
All inputs are finite; a program needn't handle non-finite values.
Results may differ from a plain program's by a relative error of at most 0.014.
Values may be sent and summed in bfloat16 or wider, within the bound.
A program may use at most 192 MiB of HBM per device.

v0:
```python
import functools
import math

import jax
import jax.numpy as jnp
from jax import lax
from jax.experimental import pallas as pl
from jax.experimental.pallas import tpu as pltpu
from jax.sharding import PartitionSpec as P

HEAD_DIM = 128
CHUNKS = 4


def nt(left, right):
    return lax.dot_general(left, right, (((1,), (1,)), ((), ())), preferred_element_type=jnp.float32)


def tn(left, right):
    return lax.dot_general(left, right, (((0,), (0,)), ((), ())), preferred_element_type=jnp.float32)


def attention_kernel(
    halos, per_group, docs, lengths, base_ref, q_ref, g_ref, k_ref, v_ref, norm_ref, dots_ref,
    dq_ref, dk_ref, dv_ref, dk_far_ref, dv_far_ref, q_stack, g_stack, dq_acc
):
    tokens = q_ref.shape[0]
    base = base_ref[0]
    scale = 1.0 / math.sqrt(HEAD_DIM)
    for j in range(per_group):
        rows = slice(j * tokens, (j + 1) * tokens)
        cols = slice(j * HEAD_DIM, (j + 1) * HEAD_DIM)
        q_stack[rows, :] = q_ref[:, cols]
        g_stack[rows, :] = g_ref[:, cols]
    query_pos = base + lax.broadcasted_iota(jnp.int32, (tokens, tokens), 1)
    key_offset = lax.broadcasted_iota(jnp.int32, (tokens, tokens), 0)
    start = jnp.zeros((tokens, tokens), jnp.int32)
    first_start = jnp.int32(0)
    end = jnp.int32(0)
    for n in range(docs):
        end = end + lengths[n]
        start = jnp.where(query_pos >= end, end, start)
        first_start = jnp.where(base >= end, end, first_start)

    def block(back):
        rows = slice((halos - back) * tokens, (halos - back + 1) * tokens)
        key_pos = base - back * tokens + key_offset
        visible = (key_pos >= start) & (key_pos <= query_pos)
        visible = jnp.concatenate([visible.astype(jnp.float32)] * per_group, axis=1)
        keys = k_ref[rows, :]
        queries = q_stack[...]
        grads = g_stack[...]
        scores = nt(keys, queries) * scale
        probs = jnp.where(visible > 0.0, jnp.exp(scores - norm_ref[0]), 0.0)
        prob_grad = nt(v_ref[rows, :], grads)
        score_grad = (probs * (prob_grad - dots_ref[0]) * scale).astype(jnp.bfloat16)
        value_part = jnp.dot(probs.astype(jnp.bfloat16), grads, preferred_element_type=jnp.float32)
        key_part = jnp.dot(score_grad, queries, preferred_element_type=jnp.float32)
        return tn(score_grad, keys), key_part, value_part

    query_part, key_part, value_part = block(0)
    dq_acc[...] = query_part
    dk_ref[...] = key_part
    dv_ref[...] = value_part
    for back in range(1, halos + 1):
        rows = slice((halos - back) * tokens, (halos - back + 1) * tokens)
        near = base - back * tokens + tokens - 1 >= first_start

        @pl.when(near)
        def _(back=back, rows=rows):
            query_part, key_part, value_part = block(back)
            dq_acc[...] += query_part
            dk_far_ref[rows, :] = key_part.astype(dk_far_ref.dtype)
            dv_far_ref[rows, :] = value_part.astype(dv_far_ref.dtype)

        @pl.when(jnp.logical_not(near))
        def _(rows=rows):
            dk_far_ref[rows, :] = jnp.zeros((tokens, HEAD_DIM), dk_far_ref.dtype)
            dv_far_ref[rows, :] = jnp.zeros((tokens, HEAD_DIM), dv_far_ref.dtype)

    for j in range(per_group):
        rows = slice(j * tokens, (j + 1) * tokens)
        dq_ref[:, j * HEAD_DIM : (j + 1) * HEAD_DIM] = dq_acc[rows, :].astype(dq_ref.dtype)


def attention(lengths, base, queries, grads, keys, values, norms, dots, halos):
    tokens = queries.shape[0]
    groups = keys.shape[1] // HEAD_DIM
    per_group = queries.shape[1] // keys.shape[1]
    wide = per_group * HEAD_DIM
    body = functools.partial(attention_kernel, halos, per_group, lengths.shape[0])
    by_group = lambda g, *_: (0, g)
    stat = pl.BlockSpec((1, 1, per_group * tokens), lambda g, *_: (g, 0, 0))
    one = jax.ShapeDtypeStruct((tokens, groups * HEAD_DIM), jnp.float32)
    far = jax.ShapeDtypeStruct((halos * tokens, groups * HEAD_DIM), jnp.bfloat16)
    return pl.pallas_call(
        body,
        grid_spec=pltpu.PrefetchScalarGridSpec(
            num_scalar_prefetch=2,
            grid=(groups,),
            in_specs=[
                pl.BlockSpec((tokens, wide), by_group),
                pl.BlockSpec((tokens, wide), by_group),
                pl.BlockSpec((keys.shape[0], HEAD_DIM), by_group),
                pl.BlockSpec((keys.shape[0], HEAD_DIM), by_group),
                stat,
                stat,
            ],
            out_specs=[
                pl.BlockSpec((tokens, wide), by_group),
                pl.BlockSpec((tokens, HEAD_DIM), by_group),
                pl.BlockSpec((tokens, HEAD_DIM), by_group),
                pl.BlockSpec((halos * tokens, HEAD_DIM), by_group),
                pl.BlockSpec((halos * tokens, HEAD_DIM), by_group),
            ],
            scratch_shapes=[
                pltpu.VMEM((per_group * tokens, HEAD_DIM), jnp.bfloat16),
                pltpu.VMEM((per_group * tokens, HEAD_DIM), jnp.bfloat16),
                pltpu.VMEM((per_group * tokens, HEAD_DIM), jnp.float32),
            ],
        ),
        out_shape=[jax.ShapeDtypeStruct(queries.shape, jnp.bfloat16), one, one, far, far],
        compiler_params=pltpu.CompilerParams(vmem_limit_bytes=40 * 1024 * 1024),
        cost_estimate=pl.CostEstimate(
            flops=30_000_000_000, bytes_accessed=10_000_000, transcendentals=3_000_000
        ),
    )(lengths, base, queries, grads, keys, values, norms, dots)


def shifted(x, by):
    blocks, halves = lax.axis_size("blk"), lax.axis_size("head")
    place = lambda i: i % halves * blocks + i // halves
    count = blocks * halves
    pairs = [(place(i), place(i + by)) for i in range(count) if 0 <= i + by < count]
    return lax.ppermute(x, ("head", "blk"), pairs)


def shards(
    queries, keys, values, attention_output, output_gradient, saved_log_normaliser, proj_grad, doc_lengths
):
    halos = lax.axis_size("head")
    queries, keys, values = queries[0], keys[0], values[0]
    outputs, grads, cols = attention_output[0], output_gradient[0], proj_grad[0]
    tokens = queries.shape[0]
    groups = keys.shape[1] // HEAD_DIM
    heads = queries.shape[1] // HEAD_DIM

    cols = lax.all_gather(cols, "head", axis=0, tiled=True)
    cols = lax.all_to_all(cols, "dp", split_axis=1, concat_axis=0, tiled=True)
    features = outputs.shape[1] // halos
    piece = features // CHUNKS
    by_half = outputs.reshape(tokens, halos, features)

    def weight(index):
        part = by_half[:, :, index * piece : (index + 1) * piece].reshape(tokens, halos * piece)
        part = lax.all_to_all(part, "head", split_axis=1, concat_axis=0, tiled=True)
        part = lax.all_gather(part, "dp", axis=0, tiled=True)
        part = tn(part, cols).astype(jnp.bfloat16)
        return lax.psum_scatter(part, "blk", scatter_dimension=1, tiled=True)

    both = jnp.concatenate([keys, values], axis=1)
    window = [shifted(both, back) for back in range(halos, 0, -1)] + [both]
    window = jnp.concatenate(window, axis=0)
    width = keys.shape[1]
    norms = lax.all_to_all(saved_log_normaliser[0], "head", split_axis=1, concat_axis=0, tiled=True)
    dots = jnp.sum(
        (grads.astype(jnp.float32) * outputs.astype(jnp.float32)).reshape(tokens, heads, HEAD_DIM), axis=2
    )
    base = (lax.axis_index("blk") * halos + lax.axis_index("head")) * tokens
    d_queries, d_keys, d_values, far_keys, far_values = attention(
        doc_lengths[0],
        base.astype(jnp.int32)[None],
        queries,
        grads,
        window[:, :width],
        window[:, width:],
        norms.reshape(groups, 1, -1),
        dots.T.reshape(groups, 1, -1),
        halos,
    )
    for back in range(1, halos + 1):
        rows = slice((halos - back) * tokens, (halos - back + 1) * tokens)
        far = shifted(jnp.concatenate([far_keys[rows], far_values[rows]], axis=1), -back)
        d_keys = d_keys + far[:, :width].astype(jnp.float32)
        d_values = d_values + far[:, width:].astype(jnp.float32)
    d_weight = jnp.concatenate([weight(index) for index in range(CHUNKS)], axis=0)
    return (
        d_queries[None],
        d_keys.astype(jnp.bfloat16)[None],
        d_values.astype(jnp.bfloat16)[None],
        d_weight,
    )


def solution(mesh):
    tokens = P("dp", ("blk", "head"), None)
    in_specs = (tokens, tokens, tokens, tokens, tokens, P("dp", "head", "blk"), tokens, P("dp", None))
    out_specs = (tokens, tokens, tokens, P("head", ("dp", "blk")))
    return jax.shard_map(shards, mesh=mesh, in_specs=in_specs, out_specs=out_specs, check_vma=False)
```

profile of v0, /device:TPU:0, one launch (start us, length us, event | category | flops | bytes accessed | tf_op | source)
XLA Modules:
  0.0 369.0 jit_solution(8114873124844151371)
XLA Ops:
  7.2 2.3 copy.26
  9.5 0.0 all-gather.13.cloned.1.call-start
  9.5 3.2 copy.24
  12.8 0.9 fusion.2
  13.7 16.0 %all_to_all.99 = bf16[128,2,1024]{0,2,1:T(8,128)(2,1)S(1)} all-to-all(bf16[128,2,1024]{0,2,1:T(8,128)(2,1)S(1)} %get-tuple-element.15), channel_id=1, replica_groups=mesh['dp'=4,'head'=2,'blk'=4] {'head'}, dimensions={1} | all-to-all | bytes 1048576 | tf_op jit(solution)/shard_map/all_to_all | solution.py:156
  29.7 1.0 copy.30
  30.8 0.0 all-gather.11.cloned.1.call-start
  30.8 15.7 %all_to_all.100 = bf16[128,2,1024]{0,2,1:T(8,128)(2,1)S(1)} all-to-all(bf16[128,2,1024]{0,2,1:T(8,128)(2,1)S(1)} %copy-done.5), channel_id=1, replica_groups=mesh['dp'=4,'head'=2,'blk'=4] {'head'}, dimensions={1} | all-to-all | bytes 1048576 | tf_op jit(solution)/shard_map/all_to_all | solution.py:156
  46.5 1.0 copy.29
  47.6 12.0 %all_to_all.101 = bf16[128,2,1024]{0,2,1:T(8,128)(2,1)S(1)} all-to-all(bf16[128,2,1024]{0,2,1:T(8,128)(2,1)S(1)} %get-tuple-element.17), channel_id=1, replica_groups=mesh['dp'=4,'head'=2,'blk'=4] {'head'}, dimensions={1} | all-to-all | bytes 1048576 | tf_op jit(solution)/shard_map/all_to_all | solution.py:156
  59.5 1.0 copy.28
  60.6 0.0 all-gather.7.cloned.1.call-start
  60.6 9.0 %all_to_all.102 = bf16[128,2,1024]{0,2,1:T(8,128)(2,1)S(1)} all-to-all(bf16[128,2,1024]{0,2,1:T(8,128)(2,1)S(1)} %get-tuple-element.14), channel_id=1, replica_groups=mesh['dp'=4,'head'=2,'blk'=4] {'head'}, dimensions={1} | all-to-all | bytes 1048576 | tf_op jit(solution)/shard_map/all_to_all | solution.py:156
  69.6 1.0 copy.25
  70.6 0.0 reduce-scatter.11.cloned.1.call-start
  70.7 37.3 %all_to_all.103 = bf16[256,4,1024]{0,2,1:T(8,128)(2,1)S(1)} all-to-all(bf16[256,4,1024]{0,2,1:T(8,128)(2,1)} %bitcast.52), channel_id=1, replica_groups=mesh['dp'=4,'head'=2,'blk'=4] {'dp'}, dimensions={1} | all-to-all | bytes 4194304 | tf_op jit(solution)/shard_map/all_to_all | solution.py:149
  108.0 2.4 copy.27
  110.4 6.0 %convolution_convert_fusion = bf16[1024,1024]{1,0:T(8,128)(2,1)} fusion(bf16[1024,1024]{1,0:T(8,128)(2,1)} %all-gather.13.cloned.1.call-done, bf16[1024,1024]{1,0:T(8,128)(2,1)} %bitcast.48), kind=kOutput, calls=%fused_computation.2 | convolution fusion | flops 2148532224 | bytes 6291456 | tf_op jit(solution)/shard_map/dot_general | solution.py:20
  116.5 1.5 copy-done.4
  118.0 5.3 %convolution_convert_fusion.1 = bf16[1024,1024]{1,0:T(8,128)(2,1)} fusion(bf16[1024,1024]{1,0:T(8,128)(2,1)} %all-gather.11.cloned.1.call-done, bf16[1024,1024]{1,0:T(8,128)(2,1)S(1)} %bitcast.50), kind=kOutput, calls=%fused_computation.3 | convolution fusion | flops 2148532224 | bytes 6291456 | tf_op jit(solution)/shard_map/dot_general | solution.py:20
  123.4 16.4 %all-gather.9.cloned.1.call-done = bf16[1024,1024]{1,0:T(8,128)(2,1)} async-done(((bf16[256,1024]{1,0:T(8,128)(2,1)}), bf16[1024,1024]{1,0:T(8,128)(2,1)}) %all-gather.9.cloned.1.call-update) | async-done | bytes 2097168 | tf_op jit(solution)/shard_map/all_gather | solution.py:157
  139.8 5.4 %convolution_convert_fusion.2 = bf16[1024,1024]{1,0:T(8,128)(2,1)} fusion(bf16[1024,1024]{1,0:T(8,128)(2,1)} %all-gather.9.cloned.1.call-done, bf16[1024,1024]{1,0:T(8,128)(2,1)S(1)} %bitcast.51), kind=kOutput, calls=%fused_computation.4 | convolution fusion | flops 2148532224 | bytes 6291456 | tf_op jit(solution)/shard_map/dot_general | solution.py:20
  145.3 4.3 %collective-permute-start.1 = (bf16[128,2048]{1,0:T(8,128)(2,1)S(1)}, bf16[128,2048]{1,0:T(8,128)(2,1)}, u32[]{:S(2)}, u32[]{:S(2)}) collective-permute-start(bf16[128,2048]{1,0:T(8,128)(2,1)S(1)} %pad_maximum_fusion.1), channel_id=1, source_target_pairs={{0,4},{4,1},{1,5},{5,2},{2,6},{6,3},{3,7},{8,12},{12,9},{9,13},{13... | collective-permute-start | bytes 1572872 | tf_op jit(solution)/shard_map/ppermute | solution.py:135
  149.7 3.4 collective-permute-start
  153.1 0.6 copy.22
  153.7 3.3 all-to-all-start
  156.9 0.2 reduce-scatter.5.cloned.1.call-start
  157.2 2.1 multiply_bitcast_fusion
  159.3 2.7 copy.31
  162.0 3.4 reduce_sum.9
  165.4 0.1 copy.23
  165.5 1.3 maximum_maximum_fusion
  166.8 1.0 fusion.3
  167.8 6.0 %convolution_convert_fusion.3 = bf16[1024,1024]{1,0:T(8,128)(2,1)} fusion(bf16[1024,1024]{1,0:T(8,128)(2,1)} %all-gather.7.cloned.1.call-done, bf16[1024,1024]{1,0:T(8,128)(2,1)} %bitcast.49), kind=kOutput, calls=%fused_computation.5 | convolution fusion | flops 2148532224 | bytes 6291456 | tf_op jit(solution)/shard_map/dot_general | solution.py:20
  173.8 0.6 copy-done.3
  174.4 1.1 copy-done.1
  175.6 1.6 copy-done.2
  177.2 7.9 %shard_map.111 = (bf16[128,8192]{1,0:T(8,128)(2,1)}, f32[128,1024]{1,0:T(8,128)S(1)}, f32[128,1024]{1,0:T(8,128)S(1)}, bf16[256,1024]{1,0:T(8,128)(2,1)S(1)}, bf16[256,1024]{1,0:T(8,128)(2,1)S(1)}) custom-call(s32[8]{0:T(128)S(1)} %bitcast.44, s32[1]{0:T(128)} %bitcast.1.base_ref, bf16[128,8192]{1,0:T(8,128)(2,1)S(1)} %bitcast.43, ...), custom_call_target="tpu_custom_call" | custom-call | flops 30000001024 | bytes 10000000 | tf_op jit(solution)/shard_map/pallas_call | solution.py:96
  185.0 0.1 fusion.4
  185.2 1.3 collective-permute-start.3
  186.5 1.3 collective-permute-start.2
  187.8 29.8 %collective-permute-done.3 = bf16[128,2048]{1,0:T(8,128)(2,1)S(1)} collective-permute-done((bf16[128,2048]{1,0:T(8,128)(2,1)S(1)}, bf16[128,2048]{1,0:T(8,128)(2,1)S(1)}, u32[]{:S(2)}, u32[]{:S(2)}) %collective-permute-start.3) | collective-permute-done | bytes 524320 | tf_op jit(solution)/shard_map/ppermute | solution.py:135
  217.6 1.0 fusion.1
  218.6 4.3 %reduce-scatter.11.cloned.1.call-done = bf16[1024,256]{1,0:T(8,128)(2,1)} async-done(((bf16[1024,1024]{1,0:T(8,128)(2,1)}), bf16[1024,256]{1,0:T(8,128)(2,1)}) %reduce-scatter.11.cloned.1.call-update) | async-done | bytes 524304 | tf_op jit(solution)/shard_map/reduce_scatter | solution.py:159
  222.9 45.5 %reduce-scatter.9.cloned.1.call-done = bf16[1024,256]{1,0:T(8,128)(2,1)} async-done(((bf16[1024,1024]{1,0:T(8,128)(2,1)}), bf16[1024,256]{1,0:T(8,128)(2,1)}) %reduce-scatter.9.cloned.1.call-update) | async-done | bytes 524304 | tf_op jit(solution)/shard_map/reduce_scatter | solution.py:159
  268.4 45.5 %reduce-scatter.7.cloned.1.call-done = bf16[1024,256]{1,0:T(8,128)(2,1)} async-done(((bf16[1024,1024]{1,0:T(8,128)(2,1)}), bf16[1024,256]{1,0:T(8,128)(2,1)}) %reduce-scatter.7.cloned.1.call-update) | async-done | bytes 524304 | tf_op jit(solution)/shard_map/reduce_scatter | solution.py:159
  313.9 45.6 %reduce-scatter.5.cloned.1.call-done = bf16[1024,256]{1,0:T(8,128)(2,1)} async-done(((bf16[1024,1024]{1,0:T(8,128)(2,1)}), bf16[1024,256]{1,0:T(8,128)(2,1)}) %reduce-scatter.5.cloned.1.call-update) | async-done | bytes 524304 | tf_op jit(solution)/shard_map/reduce_scatter | solution.py:159
  359.5 3.0 pad_maximum_fusion
  (39 shorter events, 0.5 us)
Async XLA Ops:
  7.2 63.5 %all-gather.15.cloned.1.call-start = ((), (), s32[]{:S(2)}) async-start(), calls=%async_computation.18 | async-start | bytes 3145728 | tf_op jit(solution)/shard_map/all_gather | solution.py:148
  9.5 100.9 %all-gather.13.cloned.1.call-start = ((), (), s32[]{:S(2)}) async-start(), calls=%async_computation.16 | async-start | bytes 2621440 | tf_op jit(solution)/shard_map/all_gather | solution.py:157
  13.7 17.1 %copy-start.5 = (bf16[128,2,1024]{0,2,1:T(8,128)(2,1)S(1)}, bf16[128,2,1024]{0,2,1:T(8,128)(2,1)}, u32[]{:S(2)}) copy-start(bf16[128,2,1024]{0,2,1:T(8,128)(2,1)} %get-tuple-element.16) | copy-start | bytes 1572868
  30.8 85.7 %all-gather.11.cloned.1.call-start = ((), (), s32[]{:S(2)}) async-start(), calls=%async_computation.14 | async-start | bytes 2621440 | tf_op jit(solution)/shard_map/all_gather | solution.py:157
  47.5 92.3 %all-gather.9.cloned.1.call-start = ((), (), s32[]{:S(2)}) async-start(), calls=%async_computation.12 | async-start | bytes 2621440 | tf_op jit(solution)/shard_map/all_gather | solution.py:157
  60.6 107.2 %all-gather.7.cloned.1.call-start = ((), (), s32[]{:S(2)}) async-start(), calls=%async_computation.10 | async-start | bytes 2621440 | tf_op jit(solution)/shard_map/all_gather | solution.py:157
  70.6 152.3 %reduce-scatter.11.cloned.1.call-start = ((), (), s32[]{:S(2)}) async-start(), calls=%async_computation.17 | async-start | bytes 2621440 | tf_op jit(solution)/shard_map/reduce_scatter | solution.py:159
  116.4 1.6 copy-start.4
  116.4 152.0 %reduce-scatter.9.cloned.1.call-start = ((), (), s32[]{:S(2)}) async-start(), calls=%async_computation.15 | async-start | bytes 2621440 | tf_op jit(solution)/shard_map/reduce_scatter | solution.py:159
  123.3 190.6 %reduce-scatter.7.cloned.1.call-start = ((), (), s32[]{:S(2)}) async-start(), calls=%async_computation.13 | async-start | bytes 2621440 | tf_op jit(solution)/shard_map/reduce_scatter | solution.py:159
  139.8 5.4 %copy-start.6 = (bf16[1,128,1024]{2,1,0:T(8,128)(2,1)S(1)}, bf16[1,128,1024]{2,1,0:T(8,128)(2,1)}, u32[]{:S(2)}) copy-start(bf16[1,128,1024]{2,1,0:T(8,128)(2,1)} %param.10) | copy-start | bytes 786436
  139.8 5.4 %copy-start.7 = (bf16[1,128,1024]{2,1,0:T(8,128)(2,1)S(1)}, bf16[1,128,1024]{2,1,0:T(8,128)(2,1)}, u32[]{:S(2)}) copy-start(bf16[1,128,1024]{2,1,0:T(8,128)(2,1)} %param.9) | copy-start | bytes 786436
  145.2 7.8 %copy-start.8 = (f32[1,32,256]{2,1,0:T(8,128)S(1)}, f32[1,32,256]{2,1,0:T(8,128)}, u32[]{:S(2)}) copy-start(f32[1,32,256]{2,1,0:T(8,128)} %param.13) | copy-start | bytes 98308
  145.2 11.9 %copy-start = (bf16[1,128,8192]{2,1,0:T(8,128)(2,1)S(1)}, bf16[1,128,8192]{2,1,0:T(8,128)(2,1)}, u32[]{:S(2)}) copy-start(bf16[1,128,8192]{2,1,0:T(8,128)(2,1)} %param.12) | copy-start | bytes 6291460
  145.3 20.1 %collective-permute-start.1 = (bf16[128,2048]{1,0:T(8,128)(2,1)S(1)}, bf16[128,2048]{1,0:T(8,128)(2,1)}, u32[]{:S(2)}, u32[]{:S(2)}) collective-permute-start(bf16[128,2048]{1,0:T(8,128)(2,1)S(1)} %pad_maximum_fusion.1), channel_id=1, source_target_pairs={{0,4},{4,1},{1,5},{5,2},{2,6},{6,3},{3,7},{8,12},{12,9},{9,13},{13... | collective-permute-start | bytes 1572872 | tf_op jit(solution)/shard_map/ppermute | solution.py:135
  149.7 15.8 %collective-permute-start = (bf16[128,2048]{1,0:T(8,128)(2,1)S(1)}, bf16[128,2048]{1,0:T(8,128)(2,1)}, u32[]{:S(2)}, u32[]{:S(2)}) collective-permute-start(bf16[128,2048]{1,0:T(8,128)(2,1)S(1)} %pad_maximum_fusion.1), channel_id=1, source_target_pairs={{0,1},{4,5},{1,2},{5,6},{2,3},{6,7},{8,9},{12,13},{9,10},{13,14},{... | collective-permute-start | bytes 1572872 | tf_op jit(solution)/shard_map/ppermute | solution.py:135
  153.7 20.1 %all-to-all-start = ((f32[32,2,128]{2,0,1:T(8,128)}), f32[32,2,128]{2,0,1:T(8,128)S(1)}, u32[]{:S(2)}, u32[]{:S(2)}) async-start(f32[32,2,128]{2,0,1:T(8,128)} %copy.22), calls=%async_computation | async-start | bytes 65536 | tf_op jit(solution)/shard_map/all_to_all | solution.py:165
  156.9 202.6 %reduce-scatter.5.cloned.1.call-start = ((), (), s32[]{:S(2)}) async-start(), calls=%async_computation.11 | async-start | bytes 2621440 | tf_op jit(solution)/shard_map/reduce_scatter | solution.py:159
  173.8 0.7 copy-start.3
  174.4 1.1 copy-start.1
  175.6 1.6 copy-start.2
  185.2 32.4 %collective-permute-start.3 = (bf16[128,2048]{1,0:T(8,128)(2,1)S(1)}, bf16[128,2048]{1,0:T(8,128)(2,1)S(1)}, u32[]{:S(2)}, u32[]{:S(2)}) collective-permute-start(bf16[128,2048]{1,0:T(8,128)(2,1)S(1)} %pad_maximum_fusion.3), channel_id=1, source_target_pairs={{1,0},{5,4},{2,1},{6,5},{3,2},{7,6},{9,8},{13,12},{10,9},{14,13},{... | collective-permute-start | bytes 1572872 | tf_op jit(solution)/shard_map/ppermute | solution.py:135
  186.5 31.1 %collective-permute-start.2 = (bf16[128,2048]{1,0:T(8,128)(2,1)S(1)}, bf16[128,2048]{1,0:T(8,128)(2,1)S(1)}, u32[]{:S(2)}, u32[]{:S(2)}) collective-permute-start(bf16[128,2048]{1,0:T(8,128)(2,1)S(1)} %pad_maximum_fusion.2), channel_id=1, source_target_pairs={{4,0},{1,4},{5,1},{2,5},{6,2},{3,6},{7,3},{12,8},{9,12},{13,9},{10... | collective-permute-start | bytes 1572872 | tf_op jit(solution)/shard_map/ppermute | solution.py:135
Sparse Core Ops, SparseCore 0:
  10.1 47.8 all-gather.14
  59.6 25.5 all-gather.12
  87.3 28.4 all-gather.10
  117.2 22.5 all-gather.8
  141.2 22.5 all-gather.6
  166.0 56.8 reduce-scatter.10
  225.3 43.0 reduce-scatter.8
  270.7 43.1 reduce-scatter.6
  316.3 43.1 reduce-scatter.4
where the time goes:
time: 371 us; the launch traced here: 369 us
  waiting for transfers between devices  187 us (50%)
  blocking collectives  89.9 us (24%)
  matrix products  22.7 us (6%)
  local copies, waits for them, and re-layouts  22.2 us (6%)
  starting transfers between devices  14.1 us (4%)
  between operations  14 us (4%)
  other arithmetic  10.9 us (3%)
  Pallas kernels  7.89 us (2%)
    reduce_scatter x4, waiting for transfers between devices, weight(): return lax.psum_scatter(part, 'blk', scatter_dimension=1, tiled=True)  141 us
    all_to_all x4, blocking collectives, weight(): part = lax.all_to_all(part, 'head', split_axis=1, concat_axis=0, tiled=True)  52.6 us
    all_to_all x1, blocking collectives, shards(): cols = lax.all_to_all(cols, 'dp', split_axis=1, concat_axis=0, tiled=True)  37.3 us
    ppermute x4, waiting for transfers between devices, shifted(): return lax.ppermute(x, ('head', 'blk'), pairs)  29.8 us
    dot_general x4, matrix products, tn(): lax.dot_general(left, right, (((0,), (0,)), ((), ())), preferred_element_...  22.7 us
    all_gather x4, waiting for transfers between devices, weight(): part = lax.all_gather(part, 'dp', axis=0, tiled=True)  16.5 us
    unnamed x21, local copies, waits for them, and re-layouts  13 us
    ppermute x4, starting transfers between devices, shifted(): return lax.ppermute(x, ('head', 'blk'), pairs)  10.3 us
  transfers between devices with their start and end apart: 14, of which 6 were waited for; matrix products, arithmetic and copies ran while one was open for 12% of the time, Pallas kernels for 2%

commit v1 on v0

--- a/solution.py
+++ b/solution.py
@@ -140,21 +140,53 @@
 ):
     halos = lax.axis_size("head")
     queries, keys, values = queries[0], keys[0], values[0]
-    outputs, grads, cols = attention_output[0], output_gradient[0], proj_grad[0]
+    outputs, grads, cols_own = attention_output[0], output_gradient[0], proj_grad[0]
     tokens = queries.shape[0]
     groups = keys.shape[1] // HEAD_DIM
     heads = queries.shape[1] // HEAD_DIM
 
-    cols = lax.all_gather(cols, "head", axis=0, tiled=True)
-    cols = lax.all_to_all(cols, "dp", split_axis=1, concat_axis=0, tiled=True)
+    rows_dp = lax.axis_size("dp")
+    dp_order = [0]
+    bits = [rows_dp >> n for n in range(1, rows_dp.bit_length())]
+    for bit in bits:
+        dp_order = dp_order + [other ^ bit for other in dp_order]
+    dp_index, head_index = lax.axis_index("dp"), lax.axis_index("head")
+    quarter = cols_own.shape[1] // rows_dp
     features = outputs.shape[1] // halos
     piece = features // CHUNKS
-    by_half = outputs.reshape(tokens, halos, features)
+
+    def from_head(pick):
+        return jnp.concatenate(
+            [pick(head_index)]
+            + [
+                lax.ppermute(
+                    pick((head_index + k) % halos), "head", [(i, (i + k) % halos) for i in range(halos)]
+                )
+                for k in range(1, halos)
+            ],
+            axis=0,
+        )
+
+    def flipped(x, bit):
+        return lax.ppermute(x, "dp", [(i, i ^ bit) for i in range(rows_dp)])
+
+    cols = from_head(lambda h: cols_own)
+    cols = jnp.concatenate(
+        [
+            lax.dynamic_slice_in_dim(cols, (dp_index ^ other) * quarter, quarter, 1)
+            if other == 0
+            else flipped(lax.dynamic_slice_in_dim(cols, (dp_index ^ other) * quarter, quarter, 1), other)
+            for other in dp_order
+        ],
+        axis=0,
+    )
 
     def weight(index):
-        part = by_half[:, :, index * piece : (index + 1) * piece].reshape(tokens, halos * piece)
-        part = lax.all_to_all(part, "head", split_axis=1, concat_axis=0, tiled=True)
-        part = lax.all_gather(part, "dp", axis=0, tiled=True)
+        part = from_head(
+            lambda h: lax.dynamic_slice_in_dim(outputs, h * features + index * piece, piece, 1)
+        )
+        for bit in bits:
+            part = jnp.concatenate([part, flipped(part, bit)], axis=0)
         part = tn(part, cols).astype(jnp.bfloat16)
         return lax.psum_scatter(part, "blk", scatter_dimension=1, tiled=True)
 

time: 371 us -> 297 us (0.80)
  blocking collectives: 89.9 us -> 0 us
  starting transfers between devices: 14.1 us -> 30.3 us
  waiting for transfers between devices: 187 us -> 195 us
  local copies, waits for them, and re-layouts: 22.2 us -> 16.5 us
  matrix products: 22.7 us -> 17.6 us
    ppermute x0 -> x16, waiting for transfers between devices: none -> 101 us  [the longest x11 66.3 us: flipped(): return lax.ppermute(x, 'dp', [(i, i ^ bit) for i in range(rows_dp)])]
    all_to_all x5 -> x0, blocking collectives: 89.9 us -> none  [the longest x4 52.6 us: weight(): part = lax.all_to_all(part, 'head', split_axis=1, concat_axis=0, tiled=True)]
    reduce_scatter x4, waiting for transfers between devices: 141 us -> 54.7 us  [weight(): return lax.psum_scatter(part, 'blk', scatter_dimension=1, tiled=True)]
    all_gather x5 -> x0, waiting for transfers between devices: 16.5 us -> none  [the longest x4 16.5 us: weight(): part = lax.all_gather(part, 'dp', axis=0, tiled=True)]
    ppermute x0 -> x16, starting transfers between devices: none -> 16.3 us  [the longest x5 8.23 us: from_head(): lax.ppermute(pick((head_index + k) % halos), 'head', [(i, (i + k) % halos...]
    ppermute x4, waiting for transfers between devices: 29.8 us -> 39 us  [shifted(): return lax.ppermute(x, ('head', 'blk'), pairs)]
    all_to_all x5 -> x0, local copies, waits for them, and re-layouts: 6.41 us -> none  [the longest x4 4.04 us: weight(): part = lax.all_to_all(part, 'head', split_axis=1, concat_axis=0, tiled=True)]
    dot_general x4, matrix products: 22.7 us -> 17.6 us  [tn(): lax.dot_general(left, right, (((0,), (0,)), ((), ())), preferred_element_...]
  transfers between devices with their start and end apart: 14 -> 25, of which waited for: 6 -> 17; matrix products, arithmetic and copies ran while one was open for 12% -> 10% of each run, Pallas kernels for 2% -> 3%
where the time goes in v1:
time: 297 us; the launch traced here: 296 us
  waiting for transfers between devices  195 us (66%)
  starting transfers between devices  30.3 us (10%)
  matrix products  17.6 us (6%)
  local copies, waits for them, and re-layouts  16.5 us (6%)
  other arithmetic  14.4 us (5%)
  between operations  14.2 us (5%)
  Pallas kernels  7.9 us (3%)
    ppermute x11, waiting for transfers between devices, flipped(): return lax.ppermute(x, 'dp', [(i, i ^ bit) for i in range(rows_dp)])  66.3 us
    reduce_scatter x4, waiting for transfers between devices, weight(): return lax.psum_scatter(part, 'blk', scatter_dimension=1, tiled=True)  54.7 us
    ppermute x4, waiting for transfers between devices, shifted(): return lax.ppermute(x, ('head', 'blk'), pairs)  39 us
    ppermute x5, waiting for transfers between devices, from_head(): lax.ppermute(pick((head_index + k) % halos), 'head', [(i, (i + k) % halos...  35.2 us
    dot_general x4, matrix products, tn(): lax.dot_general(left, right, (((0,), (0,)), ((), ())), preferred_element_...  17.6 us
    unnamed x61, local copies, waits for them, and re-layouts  12.1 us
    ppermute x4, starting transfers between devices, shifted(): return lax.ppermute(x, ('head', 'blk'), pairs)  10.4 us
    ppermute x5, starting transfers between devices, from_head(): lax.ppermute(pick((head_index + k) % halos), 'head', [(i, (i + k) % halos...  8.23 us
  transfers between devices with their start and end apart: 25, of which 17 were waited for; matrix products, arithmetic and copies ran while one was open for 10% of the time, Pallas kernels for 3%

profile of v1, /device:TPU:0, one launch (start us, length us, event | category | flops | bytes accessed | tf_op | source)
XLA Modules:
  0.0 296.1 jit_solution(6548253666212086673)
XLA Ops:
  7.3 2.6 dynamic-slice_bitcast_fusion.7
  9.9 2.9 collective-permute-start.17
  12.9 7.1 %collective-permute-done.17 = bf16[128,1024]{1,0:T(8,128)(2,1)S(1)} collective-permute-done((bf16[128,1024]{1,0:T(8,128)(2,1)S(1)}, bf16[128,1024]{1,0:T(8,128)(2,1)S(1)}, u32[]{:S(2)}, u32[]{:S(2)}) %collective-permute-start.17) | collective-permute-done | bytes 262176 | tf_op jit(solution)/shard_map/ppermute | solution.py:162
  20.0 2.2 collective-permute-start.18
  22.1 10.2 %collective-permute-done.18 = bf16[256,1024]{1,0:T(8,128)(2,1)S(1)} collective-permute-done((bf16[256,1024]{1,0:T(8,128)(2,1)S(1)}, bf16[256,1024]{1,0:T(8,128)(2,1)S(1)}, u32[]{:S(2)}, u32[]{:S(2)}) %collective-permute-start.18) | collective-permute-done | bytes 524320 | tf_op jit(solution)/shard_map/ppermute | solution.py:171
  33.3 8.4 %collective-permute-done.7 = bf16[128,4096]{1,0:T(8,128)(2,1)} collective-permute-done((bf16[128,4096]{1,0:T(8,128)(2,1)S(1)}, bf16[128,4096]{1,0:T(8,128)(2,1)}, u32[]{:S(2)}, u32[]{:S(2)}) %collective-permute-start.7) | collective-permute-done | bytes 1048608 | tf_op jit(solution)/shard_map/ppermute | solution.py:162
  41.7 1.4 fusion.45
  43.5 1.5 collective-permute-start.9
  45.3 11.8 %collective-permute-done.10 = bf16[256,1024]{1,0:T(8,128)(2,1)S(1)} collective-permute-done((bf16[256,1024]{1,0:T(8,128)(2,1)S(1)}, bf16[256,1024]{1,0:T(8,128)(2,1)S(1)}, u32[]{:S(2)}, u32[]{:S(2)}) %collective-permute-start.10) | collective-permute-done | bytes 524320 | tf_op jit(solution)/shard_map/ppermute | solution.py:171
  57.0 11.6 %collective-permute-done.8 = bf16[256,1024]{1,0:T(8,128)(2,1)S(1)} collective-permute-done((bf16[256,1024]{1,0:T(8,128)(2,1)S(1)}, bf16[256,1024]{1,0:T(8,128)(2,1)S(1)}, u32[]{:S(2)}, u32[]{:S(2)}) %collective-permute-start.8) | collective-permute-done | bytes 524320 | tf_op jit(solution)/shard_map/ppermute | solution.py:171
  69.4 5.0 %fusion.32 = bf16[1024,1024]{1,0:T(8,128)(2,1)} fusion(bf16[512,1024]{1,0:T(8,128)(2,1)} %collective-permute-done.19, bf16[256,1024]{1,0:T(8,128)(2,1)S(1)} %copy-done.8, bf16[128,1024]{1,0:T(8,128)(2,1)S(1)} %collective-permute-done.17, bf16[128,1024]{1,0:T(8,128)(2,1)S(1)} %get-tuple-element.21, bf16[256,1024]{1,0:T(8,128)(2,1)S(1)} %collective-permute-done.10, ...), kind=kOutput, calls=%fused_computation.43 | convolution fusion | flops 2165309440 | bytes 6291456 | tf_op jit(solution)/shard_map/dot_general | solution.py:20
  75.4 1.7 collective-permute-start.14
  77.1 6.5 %collective-permute-done.14 = bf16[128,1024]{1,0:T(8,128)(2,1)S(1)} collective-permute-done((bf16[128,1024]{1,0:T(8,128)(2,1)S(1)}, bf16[128,1024]{1,0:T(8,128)(2,1)S(1)}, u32[]{:S(2)}, u32[]{:S(2)}) %collective-permute-start.14) | collective-permute-done | bytes 262176 | tf_op jit(solution)/shard_map/ppermute | solution.py:162
  84.4 12.3 %collective-permute-done.15 = bf16[256,1024]{1,0:T(8,128)(2,1)S(1)} collective-permute-done((bf16[256,1024]{1,0:T(8,128)(2,1)S(1)}, bf16[256,1024]{1,0:T(8,128)(2,1)S(1)}, u32[]{:S(2)}, u32[]{:S(2)}) %collective-permute-start.15) | collective-permute-done | bytes 524320 | tf_op jit(solution)/shard_map/ppermute | solution.py:171
  96.9 2.6 collective-permute-done.16
  99.5 3.8 %fusion.35 = bf16[1024,1024]{1,0:T(8,128)(2,1)} fusion(bf16[512,1024]{1,0:T(8,128)(2,1)S(1)} %collective-permute-done.16, bf16[256,1024]{1,0:T(8,128)(2,1)S(1)} %collective-permute-done.15, bf16[128,1024]{1,0:T(8,128)(2,1)S(1)} %collective-permute-done.14, bf16[128,1024]{1,0:T(8,128)(2,1)S(1)} %get-tuple-element.16, bf16[256,1024]{1,0:T(8,128)(2,1)S(1)} %copy-done.19, ...), kind=kOutput, calls=%fused_computation.44 | convolution fusion | flops 2165309440 | bytes 6291456 | tf_op jit(solution)/shard_map/dot_general | solution.py:20
  104.3 1.7 collective-permute-start.11
  106.1 6.6 %collective-permute-done.11 = bf16[128,1024]{1,0:T(8,128)(2,1)S(1)} collective-permute-done((bf16[128,1024]{1,0:T(8,128)(2,1)S(1)}, bf16[128,1024]{1,0:T(8,128)(2,1)S(1)}, u32[]{:S(2)}, u32[]{:S(2)}) %collective-permute-start.11) | collective-permute-done | bytes 262176 | tf_op jit(solution)/shard_map/ppermute | solution.py:162
  112.7 1.4 collective-permute-start.12
  114.1 11.9 %collective-permute-done.12 = bf16[256,1024]{1,0:T(8,128)(2,1)S(1)} collective-permute-done((bf16[256,1024]{1,0:T(8,128)(2,1)S(1)}, bf16[256,1024]{1,0:T(8,128)(2,1)S(1)}, u32[]{:S(2)}, u32[]{:S(2)}) %collective-permute-start.12) | collective-permute-done | bytes 524320 | tf_op jit(solution)/shard_map/ppermute | solution.py:171
  126.1 2.6 collective-permute-done.13
  128.8 3.8 %fusion.38 = bf16[1024,1024]{1,0:T(8,128)(2,1)} fusion(bf16[512,1024]{1,0:T(8,128)(2,1)S(1)} %collective-permute-done.13, bf16[256,1024]{1,0:T(8,128)(2,1)S(1)} %collective-permute-done.12, bf16[128,1024]{1,0:T(8,128)(2,1)S(1)} %collective-permute-done.11, bf16[128,1024]{1,0:T(8,128)(2,1)S(1)} %get-tuple-element.18, bf16[256,1024]{1,0:T(8,128)(2,1)S(1)} %copy-done.20, ...), kind=kOutput, calls=%fused_computation.45 | convolution fusion | flops 2165309440 | bytes 6291456 | tf_op jit(solution)/shard_map/dot_general | solution.py:20
  132.7 0.9 copy-done.14
  133.6 1.7 collective-permute-start.4
  135.3 6.6 %collective-permute-done.4 = bf16[128,1024]{1,0:T(8,128)(2,1)S(1)} collective-permute-done((bf16[128,1024]{1,0:T(8,128)(2,1)S(1)}, bf16[128,1024]{1,0:T(8,128)(2,1)S(1)}, u32[]{:S(2)}, u32[]{:S(2)}) %collective-permute-start.4) | collective-permute-done | bytes 262176 | tf_op jit(solution)/shard_map/ppermute | solution.py:162
  142.0 1.4 collective-permute-start.5
  144.2 4.2 %collective-permute-start.1 = (bf16[128,2048]{1,0:T(8,128)(2,1)}, bf16[128,2048]{1,0:T(8,128)(2,1)}, u32[]{:S(2)}, u32[]{:S(2)}) collective-permute-start(bf16[128,2048]{1,0:T(8,128)(2,1)} %pad_maximum_fusion.6), channel_id=1, source_target_pairs={{0,4},{4,1},{1,5},{5,2},{2,6},{6,3},{3,7},{8,12},{12,9},{9,13},{13... | collective-permute-start | bytes 1572872 | tf_op jit(solution)/shard_map/ppermute | solution.py:135
  148.4 3.6 %collective-permute-start = (bf16[128,2048]{1,0:T(8,128)(2,1)}, bf16[128,2048]{1,0:T(8,128)(2,1)}, u32[]{:S(2)}, u32[]{:S(2)}) collective-permute-start(bf16[128,2048]{1,0:T(8,128)(2,1)} %pad_maximum_fusion.6), channel_id=1, source_target_pairs={{0,1},{4,5},{1,2},{5,6},{2,3},{6,7},{8,9},{12,13},{9,10},{13,14},{... | collective-permute-start | bytes 1572872 | tf_op jit(solution)/shard_map/ppermute | solution.py:135
  152.0 3.3 %collective-permute-done.5 = bf16[256,1024]{1,0:T(8,128)(2,1)S(1)} collective-permute-done((bf16[256,1024]{1,0:T(8,128)(2,1)S(1)}, bf16[256,1024]{1,0:T(8,128)(2,1)S(1)}, u32[]{:S(2)}, u32[]{:S(2)}) %collective-permute-start.5) | collective-permute-done | bytes 524320 | tf_op jit(solution)/shard_map/ppermute | solution.py:171
  156.1 1.0 pad_maximum_fusion.2
  157.8 3.3 %all-to-all-start = ((f32[32,2,128]{2,0,1:T(8,128)}), f32[32,2,128]{2,0,1:T(8,128)S(1)}, u32[]{:S(2)}, u32[]{:S(2)}) async-start(f32[32,2,128]{2,0,1:T(8,128)} %copy.13), calls=%async_computation | async-start | bytes 65536 | tf_op jit(solution)/shard_map/all_to_all | solution.py:197
  161.3 2.1 multiply_bitcast_fusion
  163.4 2.7 copy.15
  166.1 3.3 %reduce_sum.9 = f32[128,64]{1,0:T(8,128)S(1)} reduce(f32[128,64,128]{2,1,0:T(8,128)} %bitcast.42, f32[]{:T(128)} %constant.54.clone.1), dimensions={2}, to_apply=%region_0.0 | reduce | flops 1040384 | bytes 4227076 | tf_op jit(solution)/shard_map/reduce_sum | solution.py:198
  169.5 2.4 collective-permute-done
  171.9 1.3 maximum_maximum_fusion
  173.3 1.0 fusion.54
  175.2 5.0 %fusion.41 = bf16[1024,1024]{1,0:T(8,128)(2,1)} fusion(bf16[512,1024]{1,0:T(8,128)(2,1)} %collective-permute-done.6, bf16[256,1024]{1,0:T(8,128)(2,1)S(1)} %copy-done.10, bf16[128,1024]{1,0:T(8,128)(2,1)S(1)} %collective-permute-done.4, bf16[128,1024]{1,0:T(8,128)(2,1)S(1)} %get-tuple-element.14, bf16[256,1024]{1,0:T(8,128)(2,1)S(1)} %copy-done.21, ...), kind=kOutput, calls=%fused_computation.46 | convolution fusion | flops 2165309440 | bytes 6291456 | tf_op jit(solution)/shard_map/dot_general | solution.py:20
  180.9 1.1 copy-done.1
  182.0 1.6 copy-done.2
  183.6 7.9 %shard_map.111 = (bf16[128,8192]{1,0:T(8,128)(2,1)}, f32[128,1024]{1,0:T(8,128)S(1)}, f32[128,1024]{1,0:T(8,128)S(1)}, bf16[256,1024]{1,0:T(8,128)(2,1)S(1)}, bf16[256,1024]{1,0:T(8,128)(2,1)S(1)}) custom-call(s32[8]{0:T(128)S(1)} %bitcast.41, s32[1]{0:T(128)} %bitcast.1.base_ref, bf16[128,8192]{1,0:T(8,128)(2,1)S(1)} %bitcast.40, ...), custom_call_target="tpu_custom_call" | custom-call | flops 30000001024 | bytes 10000000 | tf_op jit(solution)/shard_map/pallas_call | solution.py:96
  191.6 1.3 collective-permute-start.3
  193.0 1.3 collective-permute-start.2
  194.3 36.6 %collective-permute-done.3 = bf16[128,2048]{1,0:T(8,128)(2,1)S(1)} collective-permute-done((bf16[128,2048]{1,0:T(8,128)(2,1)S(1)}, bf16[128,2048]{1,0:T(8,128)(2,1)S(1)}, u32[]{:S(2)}, u32[]{:S(2)}) %collective-permute-start.3) | collective-permute-done | bytes 524320 | tf_op jit(solution)/shard_map/ppermute | solution.py:135
  230.8 1.0 fusion.49
  231.9 9.6 %reduce-scatter.7.cloned.1.call-done = bf16[1024,256]{1,0:T(8,128)(2,1)} async-done(((bf16[1024,1024]{1,0:T(8,128)(2,1)}), bf16[1024,256]{1,0:T(8,128)(2,1)}) %reduce-scatter.7.cloned.1.call-update) | async-done | bytes 524304 | tf_op jit(solution)/shard_map/reduce_scatter | solution.py:191
  241.5 45.1 %reduce-scatter.5.cloned.1.call-done = bf16[1024,256]{1,0:T(8,128)(2,1)} async-done(((bf16[1024,1024]{1,0:T(8,128)(2,1)}), bf16[1024,256]{1,0:T(8,128)(2,1)}) %reduce-scatter.5.cloned.1.call-update) | async-done | bytes 524304 | tf_op jit(solution)/shard_map/reduce_scatter | solution.py:191
  286.6 3.0 %pad_maximum_fusion.1 = bf16[4096,256]{1,0:T(8,128)(2,1)} fusion(bf16[1024,256]{1,0:T(8,128)(2,1)} %reduce-scatter.11.cloned.1.call-done, bf16[1024,256]{1,0:T(8,128)(2,1)} %reduce-scatter.9.cloned.1.call-done, bf16[1024,256]{1,0:T(8,128)(2,1)} %reduce-scatter.7.cloned.1.call-done, bf16[1024,256]{1,0:T(8,128)(2,1)} %reduce-scatter.5.cloned.1.call-done), kind=kLoop, calls=%fused_computation.42 | loop fusion | flops 8388608 | bytes 4194304 | tf_op jit(solution)/shard_map/concatenate | solution.py:218
  (95 shorter events, 9.9 us)
Async XLA Ops:
  7.2 224.7 %reduce-scatter.11.cloned.1.call-start = ((), (), s32[]{:S(2)}) async-start(), calls=%async_computation.8 | async-start | bytes 2621440 | tf_op jit(solution)/shard_map/reduce_scatter | solution.py:191
  7.2 5.6 %copy-start.6 = (bf16[1,128,4096]{2,1,0:T(8,128)(2,1)S(1)}, bf16[1,128,4096]{2,1,0:T(8,128)(2,1)}, u32[]{:S(2)}) copy-start(bf16[1,128,4096]{2,1,0:T(8,128)(2,1)} %param.14) | copy-start | bytes 3145732
  9.9 10.1 %collective-permute-start.17 = (bf16[128,1024]{1,0:T(8,128)(2,1)S(1)}, bf16[128,1024]{1,0:T(8,128)(2,1)S(1)}, u32[]{:S(2)}, u32[]{:S(2)}) collective-permute-start(bf16[128,1024]{1,0:T(8,128)(2,1)S(1)} %get-tuple-element.20), channel_id=1, source_target_pairs={{0,4},{4,0},{1,5},{5,1},{2,6},{6,2},{3,7},{7,3},{8,12},{12,8},{9,1... | collective-permute-start | bytes 786440 | tf_op jit(solution)/shard_map/ppermute | solution.py:162
  12.8 28.9 %collective-permute-start.7 = (bf16[128,4096]{1,0:T(8,128)(2,1)S(1)}, bf16[128,4096]{1,0:T(8,128)(2,1)}, u32[]{:S(2)}, u32[]{:S(2)}) collective-permute-start(bf16[128,4096]{1,0:T(8,128)(2,1)S(1)} %bitcast.47), channel_id=1, source_target_pairs={{0,4},{4,0},{1,5},{5,1},{2,6},{6,2},{3,7},{7,3},{8,12},{12,8},{9,1... | collective-permute-start | bytes 3145736 | tf_op jit(solution)/shard_map/ppermute | solution.py:162
  20.0 12.3 %collective-permute-start.18 = (bf16[256,1024]{1,0:T(8,128)(2,1)S(1)}, bf16[256,1024]{1,0:T(8,128)(2,1)S(1)}, u32[]{:S(2)}, u32[]{:S(2)}) collective-permute-start(bf16[256,1024]{1,0:T(8,128)(2,1)S(1)} %pad_maximum_fusion.12), channel_id=1, source_target_pairs={{0,16},{8,24},{16,0},{24,8},{1,17},{9,25},{17,1},{25,9},{2,18},{10... | collective-permute-start | bytes 1572872 | tf_op jit(solution)/shard_map/ppermute | solution.py:171
  33.2 35.4 %collective-permute-start.19 = (bf16[512,1024]{1,0:T(8,128)(2,1)S(1)}, bf16[512,1024]{1,0:T(8,128)(2,1)}, u32[]{:S(2)}, u32[]{:S(2)}) collective-permute-start(bf16[512,1024]{1,0:T(8,128)(2,1)S(1)} %pad_maximum_fusion.5), channel_id=1, source_target_pairs={{0,8},{8,0},{16,24},{24,16},{1,9},{9,1},{17,25},{25,17},{2,10},{10... | collective-permute-start | bytes 3145736 | tf_op jit(solution)/shard_map/ppermute | solution.py:171
  33.3 36.2 %copy-start.8 = (bf16[256,1024]{1,0:T(8,128)(2,1)S(1)}, bf16[256,1024]{1,0:T(8,128)(2,1)}, u32[]{:S(2)}) copy-start(bf16[256,1024]{1,0:T(8,128)(2,1)} %copy-done.7) | copy-start | bytes 1572868
  43.0 25.5 %copy-start.11 = (bf16[256,1024]{1,0:T(8,128)(2,1)}, bf16[256,1024]{1,0:T(8,128)(2,1)S(1)}, u32[]{:S(2)}) copy-start(bf16[256,1024]{1,0:T(8,128)(2,1)S(1)} %get-tuple-element.22) | copy-start | bytes 1572868
  43.1 14.0 %collective-permute-start.10 = (bf16[256,1024]{1,0:T(8,128)(2,1)S(1)}, bf16[256,1024]{1,0:T(8,128)(2,1)S(1)}, u32[]{:S(2)}, u32[]{:S(2)}) collective-permute-start(bf16[256,1024]{1,0:T(8,128)(2,1)S(1)} %get-tuple-element.25), channel_id=1, source_target_pairs={{0,24},{8,16},{16,8},{24,0},{1,25},{9,17},{17,9},{25,1},{2,26},{10... | collective-permute-start | bytes 1572872 | tf_op jit(solution)/shard_map/ppermute | solution.py:171
  43.5 13.6 %collective-permute-start.9 = (bf16[256,1024]{1,0:T(8,128)(2,1)S(1)}, bf16[256,1024]{1,0:T(8,128)(2,1)S(1)}, u32[]{:S(2)}, u32[]{:S(2)}) collective-permute-start(bf16[256,1024]{1,0:T(8,128)(2,1)S(1)} %get-tuple-element.24), channel_id=1, source_target_pairs={{0,8},{8,0},{16,24},{24,16},{1,9},{9,1},{17,25},{25,17},{2,10},{10... | collective-permute-start | bytes 1572872 | tf_op jit(solution)/shard_map/ppermute | solution.py:171
  45.0 23.6 %collective-permute-start.8 = (bf16[256,1024]{1,0:T(8,128)(2,1)S(1)}, bf16[256,1024]{1,0:T(8,128)(2,1)S(1)}, u32[]{:S(2)}, u32[]{:S(2)}) collective-permute-start(bf16[256,1024]{1,0:T(8,128)(2,1)S(1)} %get-tuple-element.23), channel_id=1, source_target_pairs={{0,16},{8,24},{16,0},{24,8},{1,17},{9,25},{17,1},{25,9},{2,18},{10... | collective-permute-start | bytes 1572872 | tf_op jit(solution)/shard_map/ppermute | solution.py:171
  57.0 11.6 %copy-start.18 = (bf16[256,1024]{1,0:T(8,128)(2,1)}, bf16[256,1024]{1,0:T(8,128)(2,1)S(1)}, u32[]{:S(2)}) copy-start(bf16[256,1024]{1,0:T(8,128)(2,1)S(1)} %collective-permute-done.10) | copy-start | bytes 1572868
  57.0 17.4 %copy-start.22 = (bf16[256,1024]{1,0:T(8,128)(2,1)}, bf16[256,1024]{1,0:T(8,128)(2,1)S(1)}, u32[]{:S(2)}) copy-start(bf16[256,1024]{1,0:T(8,128)(2,1)S(1)} %collective-permute-done.9) | copy-start | bytes 1572868
  74.4 25.1 %copy-start.12 = (bf16[256,1024]{1,0:T(8,128)(2,1)S(1)}, bf16[256,1024]{1,0:T(8,128)(2,1)}, u32[]{:S(2)}) copy-start(bf16[256,1024]{1,0:T(8,128)(2,1)} %copy-done.11) | copy-start | bytes 1572868
  74.4 157.4 %reduce-scatter.9.cloned.1.call-start = ((), (), s32[]{:S(2)}) async-start(), calls=%async_computation.7 | async-start | bytes 2621440 | tf_op jit(solution)/shard_map/reduce_scatter | solution.py:191
  74.5 25.0 %copy-start.19 = (bf16[256,1024]{1,0:T(8,128)(2,1)S(1)}, bf16[256,1024]{1,0:T(8,128)(2,1)}, u32[]{:S(2)}) copy-start(bf16[256,1024]{1,0:T(8,128)(2,1)} %copy-done.18) | copy-start | bytes 1572868
  74.5 25.0 %copy-start.23 = (bf16[256,1024]{1,0:T(8,128)(2,1)S(1)}, bf16[256,1024]{1,0:T(8,128)(2,1)}, u32[]{:S(2)}) copy-start(bf16[256,1024]{1,0:T(8,128)(2,1)} %copy-done.22) | copy-start | bytes 1572868
  74.5 25.0 %copy-start.27 = (bf16[256,1024]{1,0:T(8,128)(2,1)S(1)}, bf16[256,1024]{1,0:T(8,128)(2,1)}, u32[]{:S(2)}) copy-start(bf16[256,1024]{1,0:T(8,128)(2,1)} %copy-done.26) | copy-start | bytes 1572868
  75.4 8.3 %collective-permute-start.14 = (bf16[128,1024]{1,0:T(8,128)(2,1)S(1)}, bf16[128,1024]{1,0:T(8,128)(2,1)S(1)}, u32[]{:S(2)}, u32[]{:S(2)}) collective-permute-start(bf16[128,1024]{1,0:T(8,128)(2,1)S(1)} %copy-done.16), channel_id=1, source_target_pairs={{0,4},{4,0},{1,5},{5,1},{2,6},{6,2},{3,7},{7,3},{8,12},{12,8},{9,1... | collective-permute-start | bytes 786440 | tf_op jit(solution)/shard_map/ppermute | solution.py:162
  83.6 13.1 %collective-permute-start.15 = (bf16[256,1024]{1,0:T(8,128)(2,1)S(1)}, bf16[256,1024]{1,0:T(8,128)(2,1)S(1)}, u32[]{:S(2)}, u32[]{:S(2)}) collective-permute-start(bf16[256,1024]{1,0:T(8,128)(2,1)S(1)} %pad_maximum_fusion.11), channel_id=1, source_target_pairs={{0,16},{8,24},{16,0},{24,8},{1,17},{9,25},{17,1},{25,9},{2,18},{10... | collective-permute-start | bytes 1572872 | tf_op jit(solution)/shard_map/ppermute | solution.py:171
  96.8 2.7 collective-permute-start.16
  103.4 138.1 %reduce-scatter.7.cloned.1.call-start = ((), (), s32[]{:S(2)}) async-start(), calls=%async_computation.6 | async-start | bytes 2621440 | tf_op jit(solution)/shard_map/reduce_scatter | solution.py:191
  103.4 25.4 %copy-start.20 = (bf16[256,1024]{1,0:T(8,128)(2,1)S(1)}, bf16[256,1024]{1,0:T(8,128)(2,1)}, u32[]{:S(2)}) copy-start(bf16[256,1024]{1,0:T(8,128)(2,1)} %copy-done.18) | copy-start | bytes 1572868
  103.4 25.4 %copy-start.24 = (bf16[256,1024]{1,0:T(8,128)(2,1)S(1)}, bf16[256,1024]{1,0:T(8,128)(2,1)}, u32[]{:S(2)}) copy-start(bf16[256,1024]{1,0:T(8,128)(2,1)} %copy-done.22) | copy-start | bytes 1572868
  103.5 25.3 %copy-start.28 = (bf16[256,1024]{1,0:T(8,128)(2,1)S(1)}, bf16[256,1024]{1,0:T(8,128)(2,1)}, u32[]{:S(2)}) copy-start(bf16[256,1024]{1,0:T(8,128)(2,1)} %copy-done.26) | copy-start | bytes 1572868
  104.3 8.3 %collective-permute-start.11 = (bf16[128,1024]{1,0:T(8,128)(2,1)S(1)}, bf16[128,1024]{1,0:T(8,128)(2,1)S(1)}, u32[]{:S(2)}, u32[]{:S(2)}) collective-permute-start(bf16[128,1024]{1,0:T(8,128)(2,1)S(1)} %copy-done.15), channel_id=1, source_target_pairs={{0,4},{4,0},{1,5},{5,1},{2,6},{6,2},{3,7},{7,3},{8,12},{12,8},{9,1... | collective-permute-start | bytes 786440 | tf_op jit(solution)/shard_map/ppermute | solution.py:162
  112.7 13.3 %collective-permute-start.12 = (bf16[256,1024]{1,0:T(8,128)(2,1)S(1)}, bf16[256,1024]{1,0:T(8,128)(2,1)S(1)}, u32[]{:S(2)}, u32[]{:S(2)}) collective-permute-start(bf16[256,1024]{1,0:T(8,128)(2,1)S(1)} %pad_maximum_fusion.10), channel_id=1, source_target_pairs={{0,16},{8,24},{16,0},{24,8},{1,17},{9,25},{17,1},{25,9},{2,18},{10... | collective-permute-start | bytes 1572872 | tf_op jit(solution)/shard_map/ppermute | solution.py:171
  126.1 2.7 collective-permute-start.13
  132.6 10.7 %copy-start.4 = (bf16[1,128,1024]{2,1,0:T(8,128)(2,1)S(1)}, bf16[1,128,1024]{2,1,0:T(8,128)(2,1)}, u32[]{:S(2)}) copy-start(bf16[1,128,1024]{2,1,0:T(8,128)(2,1)} %param.10) | copy-start | bytes 786436
  132.6 10.7 %copy-start.5 = (bf16[1,128,1024]{2,1,0:T(8,128)(2,1)S(1)}, bf16[1,128,1024]{2,1,0:T(8,128)(2,1)}, u32[]{:S(2)}) copy-start(bf16[1,128,1024]{2,1,0:T(8,128)(2,1)} %param.9) | copy-start | bytes 786436
  133.6 8.3 %collective-permute-start.4 = (bf16[128,1024]{1,0:T(8,128)(2,1)S(1)}, bf16[128,1024]{1,0:T(8,128)(2,1)S(1)}, u32[]{:S(2)}, u32[]{:S(2)}) collective-permute-start(bf16[128,1024]{1,0:T(8,128)(2,1)S(1)} %copy-done.14), channel_id=1, source_target_pairs={{0,4},{4,0},{1,5},{5,1},{2,6},{6,2},{3,7},{7,3},{8,12},{12,8},{9,1... | collective-permute-start | bytes 786440 | tf_op jit(solution)/shard_map/ppermute | solution.py:162
  141.9 15.2 %copy-start.17 = (f32[1,32,256]{2,1,0:T(8,128)S(1)}, f32[1,32,256]{2,1,0:T(8,128)}, u32[]{:S(2)}) copy-start(f32[1,32,256]{2,1,0:T(8,128)} %param.13) | copy-start | bytes 98308
  141.9 19.3 %copy-start = (bf16[1,128,8192]{2,1,0:T(8,128)(2,1)S(1)}, bf16[1,128,8192]{2,1,0:T(8,128)(2,1)}, u32[]{:S(2)}) copy-start(bf16[1,128,8192]{2,1,0:T(8,128)(2,1)} %param.12) | copy-start | bytes 6291460
  142.0 13.3 %collective-permute-start.5 = (bf16[256,1024]{1,0:T(8,128)(2,1)S(1)}, bf16[256,1024]{1,0:T(8,128)(2,1)S(1)}, u32[]{:S(2)}, u32[]{:S(2)}) collective-permute-start(bf16[256,1024]{1,0:T(8,128)(2,1)S(1)} %pad_maximum_fusion.9), channel_id=1, source_target_pairs={{0,16},{8,24},{16,0},{24,8},{1,17},{9,25},{17,1},{25,9},{2,18},{10... | collective-permute-start | bytes 1572872 | tf_op jit(solution)/shard_map/ppermute | solution.py:171
  144.2 25.3 %collective-permute-start.1 = (bf16[128,2048]{1,0:T(8,128)(2,1)}, bf16[128,2048]{1,0:T(8,128)(2,1)}, u32[]{:S(2)}, u32[]{:S(2)}) collective-permute-start(bf16[128,2048]{1,0:T(8,128)(2,1)} %pad_maximum_fusion.6), channel_id=1, source_target_pairs={{0,4},{4,1},{1,5},{5,2},{2,6},{6,3},{3,7},{8,12},{12,9},{9,13},{13... | collective-permute-start | bytes 1572872 | tf_op jit(solution)/shard_map/ppermute | solution.py:135
  148.4 23.5 %collective-permute-start = (bf16[128,2048]{1,0:T(8,128)(2,1)}, bf16[128,2048]{1,0:T(8,128)(2,1)}, u32[]{:S(2)}, u32[]{:S(2)}) collective-permute-start(bf16[128,2048]{1,0:T(8,128)(2,1)} %pad_maximum_fusion.6), channel_id=1, source_target_pairs={{0,1},{4,5},{1,2},{5,6},{2,3},{6,7},{8,9},{12,13},{9,10},{13,14},{... | collective-permute-start | bytes 1572872 | tf_op jit(solution)/shard_map/ppermute | solution.py:135
  157.1 17.2 %collective-permute-start.6 = (bf16[512,1024]{1,0:T(8,128)(2,1)}, bf16[512,1024]{1,0:T(8,128)(2,1)}, u32[]{:S(2)}, u32[]{:S(2)}) collective-permute-start(bf16[512,1024]{1,0:T(8,128)(2,1)} %pad_maximum_fusion.2), channel_id=1, source_target_pairs={{0,8},{8,0},{16,24},{24,16},{1,9},{9,1},{17,25},{25,17},{2,10},{10... | collective-permute-start | bytes 3145736 | tf_op jit(solution)/shard_map/ppermute | solution.py:171
  157.8 22.5 %all-to-all-start = ((f32[32,2,128]{2,0,1:T(8,128)}), f32[32,2,128]{2,0,1:T(8,128)S(1)}, u32[]{:S(2)}, u32[]{:S(2)}) async-start(f32[32,2,128]{2,0,1:T(8,128)} %copy.13), calls=%async_computation | async-start | bytes 65536 | tf_op jit(solution)/shard_map/all_to_all | solution.py:197
  161.0 125.5 %reduce-scatter.5.cloned.1.call-start = ((), (), s32[]{:S(2)}) async-start(), calls=%async_computation.5 | async-start | bytes 2621440 | tf_op jit(solution)/shard_map/reduce_scatter | solution.py:191
  173.3 1.1 copy-start.10
  173.3 1.5 copy-start.13
  173.3 1.6 copy-start.21
  173.3 1.8 copy-start.25
  173.3 1.9 copy-start.29
  180.9 1.1 copy-start.1
  182.0 1.6 copy-start.2
  191.6 39.2 %collective-permute-start.3 = (bf16[128,2048]{1,0:T(8,128)(2,1)S(1)}, bf16[128,2048]{1,0:T(8,128)(2,1)S(1)}, u32[]{:S(2)}, u32[]{:S(2)}) collective-permute-start(bf16[128,2048]{1,0:T(8,128)(2,1)S(1)} %pad_maximum_fusion.8), channel_id=1, source_target_pairs={{1,0},{5,4},{2,1},{6,5},{3,2},{7,6},{9,8},{13,12},{10,9},{14,13},{... | collective-permute-start | bytes 1572872 | tf_op jit(solution)/shard_map/ppermute | solution.py:135
  193.0 37.9 %collective-permute-start.2 = (bf16[128,2048]{1,0:T(8,128)(2,1)S(1)}, bf16[128,2048]{1,0:T(8,128)(2,1)S(1)}, u32[]{:S(2)}, u32[]{:S(2)}) collective-permute-start(bf16[128,2048]{1,0:T(8,128)(2,1)S(1)} %pad_maximum_fusion.7), channel_id=1, source_target_pairs={{4,0},{1,4},{5,1},{2,5},{6,2},{3,6},{7,3},{12,8},{9,12},{13,9},{10... | collective-permute-start | bytes 1572872 | tf_op jit(solution)/shard_map/ppermute | solution.py:135
  (7 other events, 6.0 us)
Sparse Core Ops, SparseCore 0:
  74.5 44.4 reduce-scatter.10
  121.4 49.7 reduce-scatter.8
  173.5 67.9 reduce-scatter.6
  243.7 42.7 reduce-scatter.4

commit v2 on v1

--- a/solution.py
+++ b/solution.py
@@ -181,14 +181,23 @@
         axis=0,
     )
 
+    mine = from_head(lambda h: lax.dynamic_slice_in_dim(outputs, h * features, features, 1))
+    blocks, block_index = lax.axis_size("blk"), lax.axis_index("blk")
+    share = quarter // blocks
+
     def weight(index):
-        part = from_head(
-            lambda h: lax.dynamic_slice_in_dim(outputs, h * features + index * piece, piece, 1)
-        )
+        part = mine[:, index * piece : (index + 1) * piece]
         for bit in bits:
             part = jnp.concatenate([part, flipped(part, bit)], axis=0)
         part = tn(part, cols).astype(jnp.bfloat16)
-        return lax.psum_scatter(part, "blk", scatter_dimension=1, tiled=True)
+        if index % 2 == 0:
+            return lax.psum_scatter(part, "blk", scatter_dimension=1, tiled=True)
+        pick = lambda b: lax.dynamic_slice_in_dim(part, b * share, share, 1)
+        total = pick(block_index).astype(jnp.float32)
+        for k in range(1, blocks):
+            pairs = [(i, (i + k) % blocks) for i in range(blocks)]
+            total += lax.ppermute(pick((block_index + k) % blocks), "blk", pairs).astype(jnp.float32)
+        return total.astype(jnp.bfloat16)
 
     both = jnp.concatenate([keys, values], axis=1)
     window = [shifted(both, back) for back in range(halos, 0, -1)] + [both]

time: 297 us -> 328 us (1.10)
  starting transfers between devices: 30.3 us -> 89.2 us
  waiting for transfers between devices: 195 us -> 164 us
  other arithmetic: 14.4 us -> 21.1 us
  local copies, waits for them, and re-layouts: 16.5 us -> 12.4 us
    ppermute x0 -> x6, waiting for transfers between devices: none -> 88.2 us  [weight(): lax.ppermute(pick((block_index + k) % blocks), 'blk', pairs)]
    ppermute x0 -> x6, starting transfers between devices: none -> 64.7 us  [weight(): lax.ppermute(pick((block_index + k) % blocks), 'blk', pairs)]
    reduce_scatter x4 -> x2, waiting for transfers between devices: 54.7 us -> 0.04 us  [weight(): return lax.psum_scatter(part, 'blk', scatter_dimension=1, tiled=True)]
    ppermute x4, waiting for transfers between devices: 39 us -> 7.01 us  [shifted(): return lax.ppermute(x, ('head', 'blk'), pairs)]
    ppermute x11, waiting for transfers between devices: 66.3 us -> 36.8 us  [flipped(): return lax.ppermute(x, 'dp', [(i, i ^ bit) for i in range(rows_dp)])]
    ppermute x5 -> x2, starting transfers between devices: 8.23 us -> 3.08 us  [from_head(): lax.ppermute(pick((head_index + k) % halos), 'head', [(i, (i + k) % halos...]
    concatenate x4, other arithmetic: 1.24 us -> 5.51 us  [weight(): part = jnp.concatenate([part, flipped(part, bit)], axis=0)]
    unnamed x61 -> x47, local copies, waits for them, and re-layouts: 12.1 us -> 8.51 us
  transfers between devices with their start and end apart: 25 -> 26, of which waited for: 17 -> 10; matrix products, arithmetic and copies ran while one was open for 10% -> 11% of each run, Pallas kernels for 3% -> 2%
where the time goes in v2:
time: 328 us; the launch traced here: 327 us
  waiting for transfers between devices  164 us (50%)
  starting transfers between devices  89.2 us (27%)
  other arithmetic  21.1 us (6%)
  matrix products  17.4 us (5%)
  between operations  14.5 us (4%)
  local copies, waits for them, and re-layouts  12.4 us (4%)
  Pallas kernels  7.9 us (2%)
    ppermute x6, waiting for transfers between devices, weight(): lax.ppermute(pick((block_index + k) % blocks), 'blk', pairs)  88.2 us
    ppermute x6, starting transfers between devices, weight(): lax.ppermute(pick((block_index + k) % blocks), 'blk', pairs)  64.7 us
    ppermute x11, waiting for transfers between devices, flipped(): return lax.ppermute(x, 'dp', [(i, i ^ bit) for i in range(rows_dp)])  36.8 us
    ppermute x2, waiting for transfers between devices, from_head(): lax.ppermute(pick((head_index + k) % halos), 'head', [(i, (i + k) % halos...  32.2 us
    dot_general x4, matrix products, tn(): lax.dot_general(left, right, (((0,), (0,)), ((), ())), preferred_element_...  17.4 us
    ppermute x4, starting transfers between devices, shifted(): return lax.ppermute(x, ('head', 'blk'), pairs)  10.7 us
    unnamed x47, local copies, waits for them, and re-layouts  8.51 us
    pallas_call x1, Pallas kernels, attention(): pl.pallas_call(body, grid_spec=pltpu.PrefetchScalarGridSpec(num_scalar_pr...  7.9 us
  transfers between devices with their start and end apart: 26, of which 10 were waited for; matrix products, arithmetic and copies ran while one was open for 11% of the time, Pallas kernels for 2%

profile of v2, /device:TPU:0, one launch (start us, length us, event | category | flops | bytes accessed | tf_op | source)
XLA Modules:
  0.0 326.8 jit_solution(12155579128234023338)
XLA Ops:
  7.2 1.7 dynamic-slice_bitcast_fusion.1
  8.9 3.0 collective-permute-start.4
  12.0 23.9 %collective-permute-done.4 = bf16[128,4096]{1,0:T(8,128)(2,1)S(1)} collective-permute-done((bf16[128,4096]{1,0:T(8,128)(2,1)S(1)}, bf16[128,4096]{1,0:T(8,128)(2,1)S(1)}, u32[]{:S(2)}, u32[]{:S(2)}) %collective-permute-start.4) | collective-permute-done | bytes 1048608 | tf_op jit(solution)/shard_map/ppermute | solution.py:162
  35.9 1.0 fusion.37
  36.9 2.1 collective-permute-start.16
  39.0 10.2 %collective-permute-done.16 = bf16[256,1024]{1,0:T(8,128)(2,1)S(1)} collective-permute-done((bf16[256,1024]{1,0:T(8,128)(2,1)S(1)}, bf16[256,1024]{1,0:T(8,128)(2,1)S(1)}, u32[]{:S(2)}, u32[]{:S(2)}) %collective-permute-start.16) | collective-permute-done | bytes 524320 | tf_op jit(solution)/shard_map/ppermute | solution.py:171
  49.4 8.3 %collective-permute-done.7 = bf16[128,4096]{1,0:T(8,128)(2,1)} collective-permute-done((bf16[128,4096]{1,0:T(8,128)(2,1)}, bf16[128,4096]{1,0:T(8,128)(2,1)}, u32[]{:S(2)}, u32[]{:S(2)}) %collective-permute-start.7) | collective-permute-done | bytes 1048608 | tf_op jit(solution)/shard_map/ppermute | solution.py:162
  57.7 1.7 fusion.40
  59.8 1.5 collective-permute-start.9
  61.6 11.8 %collective-permute-done.10 = bf16[256,1024]{1,0:T(8,128)(2,1)S(1)} collective-permute-done((bf16[256,1024]{1,0:T(8,128)(2,1)S(1)}, bf16[256,1024]{1,0:T(8,128)(2,1)S(1)}, u32[]{:S(2)}, u32[]{:S(2)}) %collective-permute-start.10) | collective-permute-done | bytes 524320 | tf_op jit(solution)/shard_map/ppermute | solution.py:171
  73.3 11.6 %collective-permute-done.8 = bf16[256,1024]{1,0:T(8,128)(2,1)S(1)} collective-permute-done((bf16[256,1024]{1,0:T(8,128)(2,1)S(1)}, bf16[256,1024]{1,0:T(8,128)(2,1)S(1)}, u32[]{:S(2)}, u32[]{:S(2)}) %collective-permute-start.8) | collective-permute-done | bytes 524320 | tf_op jit(solution)/shard_map/ppermute | solution.py:171
  84.9 0.8 copy-done.20
  85.7 5.0 %fusion.27 = bf16[1024,1024]{1,0:T(8,128)(2,1)} fusion(bf16[512,1024]{1,0:T(8,128)(2,1)} %collective-permute-done.17, bf16[256,1024]{1,0:T(8,128)(2,1)S(1)} %collective-permute-done.16, bf16[256,1024]{1,0:T(8,128)(2,1)S(1)} %get-tuple-element.17, bf16[256,1024]{1,0:T(8,128)(2,1)S(1)} %collective-permute-done.10, ...), kind=kOutput, calls=%fused_computation.42 | convolution fusion | flops 2163212288 | bytes 6291456 | tf_op jit(solution)/shard_map/dot_general | solution.py:20
  90.9 0.8 copy-done.6
  91.7 1.8 pad_maximum_fusion.7
  93.5 4.4 %collective-permute-start.1 = (bf16[128,2048]{1,0:T(8,128)(2,1)}, bf16[128,2048]{1,0:T(8,128)(2,1)}, u32[]{:S(2)}, u32[]{:S(2)}) collective-permute-start(bf16[128,2048]{1,0:T(8,128)(2,1)} %pad_maximum_fusion.7), channel_id=1, source_target_pairs={{0,4},{4,1},{1,5},{5,2},{2,6},{6,3},{3,7},{8,12},{12,9},{9,13},{13... | collective-permute-start | bytes 1572872 | tf_op jit(solution)/shard_map/ppermute | solution.py:135
  97.9 3.5 %collective-permute-start = (bf16[128,2048]{1,0:T(8,128)(2,1)}, bf16[128,2048]{1,0:T(8,128)(2,1)}, u32[]{:S(2)}, u32[]{:S(2)}) collective-permute-start(bf16[128,2048]{1,0:T(8,128)(2,1)} %pad_maximum_fusion.7), channel_id=1, source_target_pairs={{0,1},{4,5},{1,2},{5,6},{2,3},{6,7},{8,9},{12,13},{9,10},{13,14},{... | collective-permute-start | bytes 1572872 | tf_op jit(solution)/shard_map/ppermute | solution.py:135
  102.0 3.3 all-to-all-start
  105.4 2.1 pad_maximum_fusion.2
  107.5 2.1 multiply_bitcast_fusion
  109.6 2.7 copy.15
  112.3 3.4 %reduce_sum.9 = f32[128,64]{1,0:T(8,128)S(1)} reduce(f32[128,64,128]{2,1,0:T(8,128)} %bitcast.30, f32[]{:T(128)} %constant.57.clone.1), dimensions={2}, to_apply=%region_0.1 | reduce | flops 1040384 | bytes 4227076 | tf_op jit(solution)/shard_map/reduce_sum | solution.py:207
  115.8 1.3 collective-permute-start.18
  117.0 7.0 %collective-permute-done = bf16[128,2048]{1,0:T(8,128)(2,1)} collective-permute-done((bf16[128,2048]{1,0:T(8,128)(2,1)}, bf16[128,2048]{1,0:T(8,128)(2,1)}, u32[]{:S(2)}, u32[]{:S(2)}) %collective-permute-start) | collective-permute-done | bytes 524320 | tf_op jit(solution)/shard_map/ppermute | solution.py:135
  124.0 1.3 maximum_maximum_fusion
  125.4 1.0 fusion.49
  126.4 1.1 collective-permute-start.11
  127.5 3.3 collective-permute-done.18
  130.8 0.8 copy-done.8
  131.5 2.1 pad_maximum_fusion.5
  133.7 5.1 %fusion.33 = bf16[1024,1024]{1,0:T(8,128)(2,1)} fusion(bf16[512,1024]{1,0:T(8,128)(2,1)} %collective-permute-done.6, bf16[256,1024]{1,0:T(8,128)(2,1)} %collective-permute-done.5, bf16[256,1024]{1,0:T(8,128)(2,1)S(1)} %copy-done.5, bf16[256,1024]{1,0:T(8,128)(2,1)S(1)} %copy-done.15, bf16[256,1024]{1,0:T(8,128)(2,1)S(1)} %copy-done.18, ...), kind=kOutput, calls=%fused_computation.44 | convolution fusion | flops 2163212288 | bytes 6291456 | tf_op jit(solution)/shard_map/dot_general | solution.py:20
  139.5 1.1 copy-done.1
  140.6 1.6 copy-done.2
  142.2 7.9 %shard_map.111 = (bf16[128,8192]{1,0:T(8,128)(2,1)}, f32[128,1024]{1,0:T(8,128)S(1)}, f32[128,1024]{1,0:T(8,128)S(1)}, bf16[256,1024]{1,0:T(8,128)(2,1)S(1)}, bf16[256,1024]{1,0:T(8,128)(2,1)S(1)}) custom-call(s32[8]{0:T(128)S(1)} %bitcast.29, s32[1]{0:T(128)} %bitcast.1.base_ref, bf16[128,8192]{1,0:T(8,128)(2,1)S(1)} %bitcast.28, ...), custom_call_target="tpu_custom_call" | custom-call | flops 30000001024 | bytes 10000000 | tf_op jit(solution)/shard_map/pallas_call | solution.py:96
  150.2 1.3 pad_maximum_fusion.3
  152.1 1.3 collective-permute-start.3
  153.5 1.5 collective-permute-start.2
  155.0 3.8 %fusion.24 = bf16[1024,1024]{1,0:T(8,128)(2,1)S(1)} fusion(bf16[512,1024]{1,0:T(8,128)(2,1)} %collective-permute-done.19, bf16[256,1024]{1,0:T(8,128)(2,1)S(1)} %copy-done.9, bf16[256,1024]{1,0:T(8,128)(2,1)} %get-tuple-element.16, bf16[256,1024]{1,0:T(8,128)(2,1)S(1)} %copy-done.16, bf16[256,1024]{1,0:T(8,128)(2,1)S(1)} %copy-done.19, ...), kind=kOutput, calls=%fused_computation.41 | convolution fusion | flops 2163212288 | bytes 6291456 | tf_op jit(solution)/shard_map/dot_general | solution.py:20
  159.0 36.4 %collective-permute-start.22 = (bf16[1024,256]{1,0:T(8,128)(2,1)S(1)}, bf16[1024,256]{1,0:T(8,128)(2,1)S(1)}, u32[]{:S(2)}, u32[]{:S(2)}) collective-permute-start(bf16[1024,256]{1,0:T(8,128)(2,1)S(1)} %get-tuple-element.22), channel_id=1, source_target_pairs={{0,3},{1,0},{2,1},{3,2},{4,7},{5,4},{6,5},{7,6},{8,11},{9,8},{10,9... | collective-permute-start | bytes 1572872 | tf_op jit(solution)/shard_map/ppermute | solution.py:199
  196.1 3.5 %fusion.30 = bf16[1024,1024]{1,0:T(8,128)(2,1)S(1)} fusion(bf16[512,1024]{1,0:T(8,128)(2,1)S(1)} %collective-permute-done.12, bf16[256,1024]{1,0:T(8,128)(2,1)} %collective-permute-done.11, bf16[256,1024]{1,0:T(8,128)(2,1)S(1)} %get-tuple-element.15, bf16[256,1024]{1,0:T(8,128)(2,1)S(1)} %copy-done.16, bf16[256,1024]{1,0:T(8,128)(2,1)S(1)} %copy-done.19, ...), kind=kOutput, calls=%fused_computation.43 | convolution fusion | flops 2163212288 | bytes 6291456 | tf_op jit(solution)/shard_map/dot_general | solution.py:20
  199.8 3.2 collective-permute-start.15
  203.1 18.0 %collective-permute-start.14 = (bf16[1024,256]{1,0:T(8,128)(2,1)S(1)}, bf16[1024,256]{1,0:T(8,128)(2,1)S(1)}, u32[]{:S(2)}, u32[]{:S(2)}) collective-permute-start(bf16[1024,256]{1,0:T(8,128)(2,1)S(1)} %get-tuple-element.20), channel_id=1, source_target_pairs={{0,2},{1,3},{2,0},{3,1},{4,6},{5,7},{6,4},{7,5},{8,10},{9,11},{10,... | collective-permute-start | bytes 1572872 | tf_op jit(solution)/shard_map/ppermute | solution.py:199
  221.1 13.8 %collective-permute-done.22 = bf16[1024,256]{1,0:T(8,128)(2,1)S(1)} collective-permute-done((bf16[1024,256]{1,0:T(8,128)(2,1)S(1)}, bf16[1024,256]{1,0:T(8,128)(2,1)S(1)}, u32[]{:S(2)}, u32[]{:S(2)}) %collective-permute-start.22) | collective-permute-done | bytes 524320 | tf_op jit(solution)/shard_map/ppermute | solution.py:199
  234.9 6.4 %collective-permute-start.13 = (bf16[1024,256]{1,0:T(8,128)(2,1)S(1)}, bf16[1024,256]{1,0:T(8,128)(2,1)S(1)}, u32[]{:S(2)}, u32[]{:S(2)}) collective-permute-start(bf16[1024,256]{1,0:T(8,128)(2,1)S(1)} %get-tuple-element.18), channel_id=1, source_target_pairs={{0,1},{1,2},{2,3},{3,0},{4,5},{5,6},{6,7},{7,4},{8,9},{9,10},{10,1... | collective-permute-start | bytes 1572872 | tf_op jit(solution)/shard_map/ppermute | solution.py:199
  241.3 1.1 fusion.44
  242.3 30.3 %collective-permute-done.21 = bf16[1024,256]{1,0:T(8,128)(2,1)S(1)} collective-permute-done((bf16[1024,256]{1,0:T(8,128)(2,1)S(1)}, bf16[1024,256]{1,0:T(8,128)(2,1)S(1)}, u32[]{:S(2)}, u32[]{:S(2)}) %collective-permute-start.21) | collective-permute-done | bytes 524320 | tf_op jit(solution)/shard_map/ppermute | solution.py:199
  272.9 44.0 %collective-permute-done.14 = bf16[1024,256]{1,0:T(8,128)(2,1)S(1)} collective-permute-done((bf16[1024,256]{1,0:T(8,128)(2,1)S(1)}, bf16[1024,256]{1,0:T(8,128)(2,1)S(1)}, u32[]{:S(2)}, u32[]{:S(2)}) %collective-permute-start.14) | collective-permute-done | bytes 524320 | tf_op jit(solution)/shard_map/ppermute | solution.py:199
  317.3 2.7 pad_maximum_fusion.1
  (82 shorter events, 5.0 us)
Async XLA Ops:
  7.2 310.1 %reduce-scatter.5.cloned.1.call-start = ((), (), s32[]{:S(2)}) async-start(), calls=%async_computation.4 | async-start | bytes 2621440 | tf_op jit(solution)/shard_map/reduce_scatter | solution.py:194
  8.9 27.0 %collective-permute-start.4 = (bf16[128,4096]{1,0:T(8,128)(2,1)S(1)}, bf16[128,4096]{1,0:T(8,128)(2,1)S(1)}, u32[]{:S(2)}, u32[]{:S(2)}) collective-permute-start(bf16[128,4096]{1,0:T(8,128)(2,1)S(1)} %get-tuple-element.29), channel_id=1, source_target_pairs={{0,4},{4,0},{1,5},{5,1},{2,6},{6,2},{3,7},{7,3},{8,12},{12,8},{9,1... | collective-permute-start | bytes 3145736 | tf_op jit(solution)/shard_map/ppermute | solution.py:162
  11.9 45.7 %collective-permute-start.7 = (bf16[128,4096]{1,0:T(8,128)(2,1)}, bf16[128,4096]{1,0:T(8,128)(2,1)}, u32[]{:S(2)}, u32[]{:S(2)}) collective-permute-start(bf16[128,4096]{1,0:T(8,128)(2,1)} %bitcast.15), channel_id=1, source_target_pairs={{0,4},{4,0},{1,5},{5,1},{2,6},{6,2},{3,7},{7,3},{8,12},{12,8},{9,1... | collective-permute-start | bytes 3145736 | tf_op jit(solution)/shard_map/ppermute | solution.py:162
  36.9 68.5 %copy-start.4 = (bf16[256,1024]{1,0:T(8,128)(2,1)}, bf16[256,1024]{1,0:T(8,128)(2,1)S(1)}, u32[]{:S(2)}) copy-start(bf16[256,1024]{1,0:T(8,128)(2,1)S(1)} %get-tuple-element.14) | copy-start | bytes 1572868
  36.9 12.3 %collective-permute-start.16 = (bf16[256,1024]{1,0:T(8,128)(2,1)S(1)}, bf16[256,1024]{1,0:T(8,128)(2,1)S(1)}, u32[]{:S(2)}, u32[]{:S(2)}) collective-permute-start(bf16[256,1024]{1,0:T(8,128)(2,1)S(1)} %get-tuple-element.17), channel_id=1, source_target_pairs={{0,16},{8,24},{16,0},{24,8},{1,17},{9,25},{17,1},{25,9},{2,18},{10... | collective-permute-start | bytes 1572872 | tf_op jit(solution)/shard_map/ppermute | solution.py:171
  49.3 35.6 %collective-permute-start.17 = (bf16[512,1024]{1,0:T(8,128)(2,1)S(1)}, bf16[512,1024]{1,0:T(8,128)(2,1)}, u32[]{:S(2)}, u32[]{:S(2)}) collective-permute-start(bf16[512,1024]{1,0:T(8,128)(2,1)S(1)} %pad_maximum_fusion.4), channel_id=1, source_target_pairs={{0,8},{8,0},{16,24},{24,16},{1,9},{9,1},{17,25},{25,17},{2,10},{10... | collective-permute-start | bytes 3145736 | tf_op jit(solution)/shard_map/ppermute | solution.py:171
  59.4 25.5 %copy-start.10 = (bf16[256,1024]{1,0:T(8,128)(2,1)}, bf16[256,1024]{1,0:T(8,128)(2,1)S(1)}, u32[]{:S(2)}) copy-start(bf16[256,1024]{1,0:T(8,128)(2,1)S(1)} %get-tuple-element.24) | copy-start | bytes 1572868
  59.4 14.0 %collective-permute-start.10 = (bf16[256,1024]{1,0:T(8,128)(2,1)S(1)}, bf16[256,1024]{1,0:T(8,128)(2,1)S(1)}, u32[]{:S(2)}, u32[]{:S(2)}) collective-permute-start(bf16[256,1024]{1,0:T(8,128)(2,1)S(1)} %get-tuple-element.27), channel_id=1, source_target_pairs={{0,24},{8,16},{16,8},{24,0},{1,25},{9,17},{17,9},{25,1},{2,26},{10... | collective-permute-start | bytes 1572872 | tf_op jit(solution)/shard_map/ppermute | solution.py:171
  59.8 13.6 %collective-permute-start.9 = (bf16[256,1024]{1,0:T(8,128)(2,1)S(1)}, bf16[256,1024]{1,0:T(8,128)(2,1)S(1)}, u32[]{:S(2)}, u32[]{:S(2)}) collective-permute-start(bf16[256,1024]{1,0:T(8,128)(2,1)S(1)} %get-tuple-element.26), channel_id=1, source_target_pairs={{0,8},{8,0},{16,24},{24,16},{1,9},{9,1},{17,25},{25,17},{2,10},{10... | collective-permute-start | bytes 1572872 | tf_op jit(solution)/shard_map/ppermute | solution.py:171
  61.3 23.6 %collective-permute-start.8 = (bf16[256,1024]{1,0:T(8,128)(2,1)S(1)}, bf16[256,1024]{1,0:T(8,128)(2,1)S(1)}, u32[]{:S(2)}, u32[]{:S(2)}) collective-permute-start(bf16[256,1024]{1,0:T(8,128)(2,1)S(1)} %get-tuple-element.25), channel_id=1, source_target_pairs={{0,16},{8,24},{16,0},{24,8},{1,17},{9,25},{17,1},{25,9},{2,18},{10... | collective-permute-start | bytes 1572872 | tf_op jit(solution)/shard_map/ppermute | solution.py:171
  73.3 11.6 %copy-start.14 = (bf16[256,1024]{1,0:T(8,128)(2,1)}, bf16[256,1024]{1,0:T(8,128)(2,1)S(1)}, u32[]{:S(2)}) copy-start(bf16[256,1024]{1,0:T(8,128)(2,1)S(1)} %collective-permute-done.10) | copy-start | bytes 1572868
  73.3 11.6 %copy-start.17 = (bf16[256,1024]{1,0:T(8,128)(2,1)}, bf16[256,1024]{1,0:T(8,128)(2,1)S(1)}, u32[]{:S(2)}) copy-start(bf16[256,1024]{1,0:T(8,128)(2,1)S(1)} %collective-permute-done.9) | copy-start | bytes 1572868
  84.9 0.8 copy-start.20
  90.7 0.9 copy-start.6
  90.7 10.7 %copy-start.13 = (f32[1,32,256]{2,1,0:T(8,128)S(1)}, f32[1,32,256]{2,1,0:T(8,128)}, u32[]{:S(2)}) copy-start(f32[1,32,256]{2,1,0:T(8,128)} %param.13) | copy-start | bytes 98308
  90.7 16.8 %copy-start = (bf16[1,128,8192]{2,1,0:T(8,128)(2,1)S(1)}, bf16[1,128,8192]{2,1,0:T(8,128)(2,1)}, u32[]{:S(2)}) copy-start(bf16[1,128,8192]{2,1,0:T(8,128)(2,1)} %param.12) | copy-start | bytes 6291460
  90.8 14.6 %collective-permute-start.5 = (bf16[256,1024]{1,0:T(8,128)(2,1)S(1)}, bf16[256,1024]{1,0:T(8,128)(2,1)}, u32[]{:S(2)}, u32[]{:S(2)}) collective-permute-start(bf16[256,1024]{1,0:T(8,128)(2,1)S(1)} %get-tuple-element.14), channel_id=1, source_target_pairs={{0,16},{8,24},{16,0},{24,8},{1,17},{9,25},{17,1},{25,9},{2,18},{10... | collective-permute-start | bytes 1572872 | tf_op jit(solution)/shard_map/ppermute | solution.py:171
  93.5 23.5 %collective-permute-start.1 = (bf16[128,2048]{1,0:T(8,128)(2,1)}, bf16[128,2048]{1,0:T(8,128)(2,1)}, u32[]{:S(2)}, u32[]{:S(2)}) collective-permute-start(bf16[128,2048]{1,0:T(8,128)(2,1)} %pad_maximum_fusion.7), channel_id=1, source_target_pairs={{0,4},{4,1},{1,5},{5,2},{2,6},{6,3},{3,7},{8,12},{12,9},{9,13},{13... | collective-permute-start | bytes 1572872 | tf_op jit(solution)/shard_map/ppermute | solution.py:135
  97.9 26.1 %collective-permute-start = (bf16[128,2048]{1,0:T(8,128)(2,1)}, bf16[128,2048]{1,0:T(8,128)(2,1)}, u32[]{:S(2)}, u32[]{:S(2)}) collective-permute-start(bf16[128,2048]{1,0:T(8,128)(2,1)} %pad_maximum_fusion.7), channel_id=1, source_target_pairs={{0,1},{4,5},{1,2},{5,6},{2,3},{6,7},{8,9},{12,13},{9,10},{13,14},{... | collective-permute-start | bytes 1572872 | tf_op jit(solution)/shard_map/ppermute | solution.py:135
  102.0 36.8 %all-to-all-start = ((f32[32,2,128]{2,0,1:T(8,128)}), f32[32,2,128]{2,0,1:T(8,128)S(1)}, u32[]{:S(2)}, u32[]{:S(2)}) async-start(f32[32,2,128]{2,0,1:T(8,128)} %copy.13), calls=%async_computation | async-start | bytes 65536 | tf_op jit(solution)/shard_map/all_to_all | solution.py:206
  105.3 212.0 %reduce-scatter.3.cloned.1.call-start = ((), (), s32[]{:S(2)}) async-start(), calls=%async_computation.3 | async-start | bytes 2621440 | tf_op jit(solution)/shard_map/reduce_scatter | solution.py:194
  107.5 26.1 %collective-permute-start.6 = (bf16[512,1024]{1,0:T(8,128)(2,1)}, bf16[512,1024]{1,0:T(8,128)(2,1)}, u32[]{:S(2)}, u32[]{:S(2)}) collective-permute-start(bf16[512,1024]{1,0:T(8,128)(2,1)} %pad_maximum_fusion.2), channel_id=1, source_target_pairs={{0,8},{8,0},{16,24},{24,16},{1,9},{9,1},{17,25},{25,17},{2,10},{10... | collective-permute-start | bytes 3145736 | tf_op jit(solution)/shard_map/ppermute | solution.py:171
  112.3 11.7 %copy-start.7 = (bf16[1,128,1024]{2,1,0:T(8,128)(2,1)S(1)}, bf16[1,128,1024]{2,1,0:T(8,128)(2,1)}, u32[]{:S(2)}) copy-start(bf16[1,128,1024]{2,1,0:T(8,128)(2,1)} %param.9) | copy-start | bytes 786436
  115.8 15.0 %collective-permute-start.18 = (bf16[256,1024]{1,0:T(8,128)(2,1)}, bf16[256,1024]{1,0:T(8,128)(2,1)S(1)}, u32[]{:S(2)}, u32[]{:S(2)}) collective-permute-start(bf16[256,1024]{1,0:T(8,128)(2,1)} %get-tuple-element.16), channel_id=1, source_target_pairs={{0,16},{8,24},{16,0},{24,8},{1,17},{9,25},{17,1},{25,9},{2,18},{10... | collective-permute-start | bytes 1572872 | tf_op jit(solution)/shard_map/ppermute | solution.py:171
  125.3 8.3 %copy-start.5 = (bf16[256,1024]{1,0:T(8,128)(2,1)S(1)}, bf16[256,1024]{1,0:T(8,128)(2,1)}, u32[]{:S(2)}) copy-start(bf16[256,1024]{1,0:T(8,128)(2,1)} %copy-done.4) | copy-start | bytes 1572868
  125.3 8.3 %copy-start.11 = (bf16[256,1024]{1,0:T(8,128)(2,1)S(1)}, bf16[256,1024]{1,0:T(8,128)(2,1)}, u32[]{:S(2)}) copy-start(bf16[256,1024]{1,0:T(8,128)(2,1)} %copy-done.10) | copy-start | bytes 1572868
  125.4 8.3 %copy-start.15 = (bf16[256,1024]{1,0:T(8,128)(2,1)S(1)}, bf16[256,1024]{1,0:T(8,128)(2,1)}, u32[]{:S(2)}) copy-start(bf16[256,1024]{1,0:T(8,128)(2,1)} %copy-done.14) | copy-start | bytes 1572868
  125.4 8.3 %copy-start.18 = (bf16[256,1024]{1,0:T(8,128)(2,1)S(1)}, bf16[256,1024]{1,0:T(8,128)(2,1)}, u32[]{:S(2)}) copy-start(bf16[256,1024]{1,0:T(8,128)(2,1)} %copy-done.17) | copy-start | bytes 1572868
  125.4 8.3 %copy-start.21 = (bf16[256,1024]{1,0:T(8,128)(2,1)S(1)}, bf16[256,1024]{1,0:T(8,128)(2,1)}, u32[]{:S(2)}) copy-start(bf16[256,1024]{1,0:T(8,128)(2,1)} %copy-done.20) | copy-start | bytes 1572868
  126.4 23.8 %collective-permute-start.11 = (bf16[256,1024]{1,0:T(8,128)(2,1)S(1)}, bf16[256,1024]{1,0:T(8,128)(2,1)}, u32[]{:S(2)}, u32[]{:S(2)}) collective-permute-start(bf16[256,1024]{1,0:T(8,128)(2,1)S(1)} %get-tuple-element.15), channel_id=1, source_target_pairs={{0,16},{8,24},{16,0},{24,8},{1,17},{9,25},{17,1},{25,9},{2,18},{10... | collective-permute-start | bytes 1572872 | tf_op jit(solution)/shard_map/ppermute | solution.py:171
  130.8 0.8 copy-start.8
  133.6 21.3 %collective-permute-start.19 = (bf16[512,1024]{1,0:T(8,128)(2,1)}, bf16[512,1024]{1,0:T(8,128)(2,1)}, u32[]{:S(2)}, u32[]{:S(2)}) collective-permute-start(bf16[512,1024]{1,0:T(8,128)(2,1)} %pad_maximum_fusion.5), channel_id=1, source_target_pairs={{0,8},{8,0},{16,24},{24,16},{1,9},{9,1},{17,25},{25,17},{2,10},{10... | collective-permute-start | bytes 3145736 | tf_op jit(solution)/shard_map/ppermute | solution.py:171
  139.5 1.1 copy-start.1
  140.6 1.6 copy-start.2
  150.2 4.8 %copy-start.9 = (bf16[256,1024]{1,0:T(8,128)(2,1)S(1)}, bf16[256,1024]{1,0:T(8,128)(2,1)}, u32[]{:S(2)}) copy-start(bf16[256,1024]{1,0:T(8,128)(2,1)} %copy-done.8) | copy-start | bytes 1572868
  150.2 4.8 %copy-start.12 = (bf16[256,1024]{1,0:T(8,128)(2,1)S(1)}, bf16[256,1024]{1,0:T(8,128)(2,1)}, u32[]{:S(2)}) copy-start(bf16[256,1024]{1,0:T(8,128)(2,1)} %copy-done.10) | copy-start | bytes 1572868
  150.2 4.8 %copy-start.16 = (bf16[256,1024]{1,0:T(8,128)(2,1)S(1)}, bf16[256,1024]{1,0:T(8,128)(2,1)}, u32[]{:S(2)}) copy-start(bf16[256,1024]{1,0:T(8,128)(2,1)} %copy-done.14) | copy-start | bytes 1572868
  150.2 4.8 %copy-start.19 = (bf16[256,1024]{1,0:T(8,128)(2,1)S(1)}, bf16[256,1024]{1,0:T(8,128)(2,1)}, u32[]{:S(2)}) copy-start(bf16[256,1024]{1,0:T(8,128)(2,1)} %copy-done.17) | copy-start | bytes 1572868
  150.2 4.8 %copy-start.22 = (bf16[256,1024]{1,0:T(8,128)(2,1)S(1)}, bf16[256,1024]{1,0:T(8,128)(2,1)}, u32[]{:S(2)}) copy-start(bf16[256,1024]{1,0:T(8,128)(2,1)} %copy-done.20) | copy-start | bytes 1572868
  151.5 44.0 %collective-permute-start.12 = (bf16[512,1024]{1,0:T(8,128)(2,1)S(1)}, bf16[512,1024]{1,0:T(8,128)(2,1)S(1)}, u32[]{:S(2)}, u32[]{:S(2)}) collective-permute-start(bf16[512,1024]{1,0:T(8,128)(2,1)S(1)} %pad_maximum_fusion.3), channel_id=1, source_target_pairs={{0,8},{8,0},{16,24},{24,16},{1,9},{9,1},{17,25},{25,17},{2,10},{10... | collective-permute-start | bytes 3145736 | tf_op jit(solution)/shard_map/ppermute | solution.py:171
  152.1 47.7 %collective-permute-start.3 = (bf16[128,2048]{1,0:T(8,128)(2,1)S(1)}, bf16[128,2048]{1,0:T(8,128)(2,1)S(1)}, u32[]{:S(2)}, u32[]{:S(2)}) collective-permute-start(bf16[128,2048]{1,0:T(8,128)(2,1)S(1)} %pad_maximum_fusion.9), channel_id=1, source_target_pairs={{1,0},{5,4},{2,1},{6,5},{3,2},{7,6},{9,8},{13,12},{10,9},{14,13},{... | collective-permute-start | bytes 1572872 | tf_op jit(solution)/shard_map/ppermute | solution.py:135
  153.5 49.6 %collective-permute-start.2 = (bf16[128,2048]{1,0:T(8,128)(2,1)S(1)}, bf16[128,2048]{1,0:T(8,128)(2,1)S(1)}, u32[]{:S(2)}, u32[]{:S(2)}) collective-permute-start(bf16[128,2048]{1,0:T(8,128)(2,1)S(1)} %pad_maximum_fusion.8), channel_id=1, source_target_pairs={{4,0},{1,4},{5,1},{2,5},{6,2},{3,6},{7,3},{12,8},{9,12},{13,9},{10... | collective-permute-start | bytes 1572872 | tf_op jit(solution)/shard_map/ppermute | solution.py:135
  159.0 75.9 %collective-permute-start.22 = (bf16[1024,256]{1,0:T(8,128)(2,1)S(1)}, bf16[1024,256]{1,0:T(8,128)(2,1)S(1)}, u32[]{:S(2)}, u32[]{:S(2)}) collective-permute-start(bf16[1024,256]{1,0:T(8,128)(2,1)S(1)} %get-tuple-element.22), channel_id=1, source_target_pairs={{0,3},{1,0},{2,1},{3,2},{4,7},{5,4},{6,5},{7,6},{8,11},{9,8},{10,9... | collective-permute-start | bytes 1572872 | tf_op jit(solution)/shard_map/ppermute | solution.py:199
  195.5 77.2 %collective-permute-start.21 = (bf16[1024,256]{1,0:T(8,128)(2,1)S(1)}, bf16[1024,256]{1,0:T(8,128)(2,1)S(1)}, u32[]{:S(2)}, u32[]{:S(2)}) collective-permute-start(bf16[1024,256]{1,0:T(8,128)(2,1)S(1)} %get-tuple-element.23), channel_id=1, source_target_pairs={{0,2},{1,3},{2,0},{3,1},{4,6},{5,7},{6,4},{7,5},{8,10},{9,11},{10,... | collective-permute-start | bytes 1572872 | tf_op jit(solution)/shard_map/ppermute | solution.py:199
  195.5 77.2 %collective-permute-start.20 = (bf16[1024,256]{1,0:T(8,128)(2,1)S(1)}, bf16[1024,256]{1,0:T(8,128)(2,1)S(1)}, u32[]{:S(2)}, u32[]{:S(2)}) collective-permute-start(bf16[1024,256]{1,0:T(8,128)(2,1)S(1)} %get-tuple-element.21), channel_id=1, source_target_pairs={{0,1},{1,2},{2,3},{3,0},{4,5},{5,6},{6,7},{7,4},{8,9},{9,10},{10,1... | collective-permute-start | bytes 1572872 | tf_op jit(solution)/shard_map/ppermute | solution.py:199
  199.8 73.1 %collective-permute-start.15 = (bf16[1024,256]{1,0:T(8,128)(2,1)S(1)}, bf16[1024,256]{1,0:T(8,128)(2,1)S(1)}, u32[]{:S(2)}, u32[]{:S(2)}) collective-permute-start(bf16[1024,256]{1,0:T(8,128)(2,1)S(1)} %get-tuple-element.19), channel_id=1, source_target_pairs={{0,3},{1,0},{2,1},{3,2},{4,7},{5,4},{6,5},{7,6},{8,11},{9,8},{10,9... | collective-permute-start | bytes 1572872 | tf_op jit(solution)/shard_map/ppermute | solution.py:199
  203.1 113.9 %collective-permute-start.14 = (bf16[1024,256]{1,0:T(8,128)(2,1)S(1)}, bf16[1024,256]{1,0:T(8,128)(2,1)S(1)}, u32[]{:S(2)}, u32[]{:S(2)}) collective-permute-start(bf16[1024,256]{1,0:T(8,128)(2,1)S(1)} %get-tuple-element.20), channel_id=1, source_target_pairs={{0,2},{1,3},{2,0},{3,1},{4,6},{5,7},{6,4},{7,5},{8,10},{9,11},{10,... | collective-permute-start | bytes 1572872 | tf_op jit(solution)/shard_map/ppermute | solution.py:199
  234.9 82.1 %collective-permute-start.13 = (bf16[1024,256]{1,0:T(8,128)(2,1)S(1)}, bf16[1024,256]{1,0:T(8,128)(2,1)S(1)}, u32[]{:S(2)}, u32[]{:S(2)}) collective-permute-start(bf16[1024,256]{1,0:T(8,128)(2,1)S(1)} %get-tuple-element.18), channel_id=1, source_target_pairs={{0,1},{1,2},{2,3},{3,0},{4,5},{5,6},{6,7},{7,4},{8,9},{9,10},{10,1... | collective-permute-start | bytes 1572872 | tf_op jit(solution)/shard_map/ppermute | solution.py:199
  (1 other events, 0.7 us)
Sparse Core Ops, SparseCore 0:
  90.9 52.7 reduce-scatter.4
  146.1 93.9 reduce-scatter.2

commit v3 on v1

--- a/solution.py
+++ b/solution.py
@@ -155,7 +155,7 @@
     features = outputs.shape[1] // halos
     piece = features // CHUNKS
 
-    def from_head(pick):
+    def from_head(pick, head_index):
         return jnp.concatenate(
             [pick(head_index)]
             + [
@@ -170,7 +170,7 @@
     def flipped(x, bit):
         return lax.ppermute(x, "dp", [(i, i ^ bit) for i in range(rows_dp)])
 
-    cols = from_head(lambda h: cols_own)
+    cols = from_head(lambda h: cols_own, head_index)
     cols = jnp.concatenate(
         [
             lax.dynamic_slice_in_dim(cols, (dp_index ^ other) * quarter, quarter, 1)
@@ -181,9 +181,10 @@
         axis=0,
     )
 
-    def weight(index):
+    def weight(index, head_index):
         part = from_head(
-            lambda h: lax.dynamic_slice_in_dim(outputs, h * features + index * piece, piece, 1)
+            lambda h: lax.dynamic_slice_in_dim(outputs, h * features + index * piece, piece, 1),
+            head_index,
         )
         for bit in bits:
             part = jnp.concatenate([part, flipped(part, bit)], axis=0)
@@ -210,12 +211,15 @@
         dots.T.reshape(groups, 1, -1),
         halos,
     )
+    second_index, far_keys, far_values = lax.optimization_barrier((head_index, far_keys, far_values))
     for back in range(1, halos + 1):
         rows = slice((halos - back) * tokens, (halos - back + 1) * tokens)
         far = shifted(jnp.concatenate([far_keys[rows], far_values[rows]], axis=1), -back)
         d_keys = d_keys + far[:, :width].astype(jnp.float32)
         d_values = d_values + far[:, width:].astype(jnp.float32)
-    d_weight = jnp.concatenate([weight(index) for index in range(CHUNKS)], axis=0)
+    later_index, d_keys, d_values = lax.optimization_barrier((second_index, d_keys, d_values))
+    chosen = [head_index, second_index] + [later_index] * (CHUNKS - 2)
+    d_weight = jnp.concatenate([weight(index, chosen[index]) for index in range(CHUNKS)], axis=0)
     return (
         d_queries[None],
         d_keys.astype(jnp.bfloat16)[None],

time: 297 us -> 333 us (1.12)
  waiting for transfers between devices: 195 us -> 226 us
  starting transfers between devices: 30.3 us -> 36.7 us
    reduce_scatter x4, waiting for transfers between devices: 54.7 us -> 95.5 us  [weight(): return lax.psum_scatter(part, 'blk', scatter_dimension=1, tiled=True)]
    ppermute x4, waiting for transfers between devices: 39 us -> 23.2 us  [shifted(): return lax.ppermute(x, ('head', 'blk'), pairs)]
    ppermute x11, waiting for transfers between devices: 66.3 us -> 76.5 us  [flipped(): return lax.ppermute(x, 'dp', [(i, i ^ bit) for i in range(rows_dp)])]
    ppermute x11, starting transfers between devices: 8.08 us -> 12.2 us  [flipped(): return lax.ppermute(x, 'dp', [(i, i ^ bit) for i in range(rows_dp)])]
    ppermute x5, waiting for transfers between devices: 35.2 us -> 31.2 us  [from_head(): lax.ppermute(pick((head_index + k) % halos), 'head', [(i, (i + k) % halos...]
    unnamed x61 -> x51, local copies, waits for them, and re-layouts: 12.1 us -> 10.3 us
  transfers between devices with their start and end apart: 25 -> 25, of which waited for: 17 -> 19; matrix products, arithmetic and copies ran while one was open for 10% -> 7% of each run, Pallas kernels for 3% -> 0%
where the time goes in v3:
time: 333 us; the launch traced here: 331 us
  waiting for transfers between devices  226 us (68%)
  starting transfers between devices  36.7 us (11%)
  matrix products  16.2 us (5%)
  other arithmetic  16.1 us (5%)
  between operations  14.1 us (4%)
  local copies, waits for them, and re-layouts  13.9 us (4%)
  Pallas kernels  7.9 us (2%)
    reduce_scatter x4, waiting for transfers between devices, weight(): return lax.psum_scatter(part, 'blk', scatter_dimension=1, tiled=True)  95.5 us
    ppermute x11, waiting for transfers between devices, flipped(): return lax.ppermute(x, 'dp', [(i, i ^ bit) for i in range(rows_dp)])  76.5 us
    ppermute x5, waiting for transfers between devices, from_head(): lax.ppermute(pick((head_index + k) % halos), 'head', [(i, (i + k) % halos...  31.2 us
    ppermute x4, waiting for transfers between devices, shifted(): return lax.ppermute(x, ('head', 'blk'), pairs)  23.2 us
    dot_general x4, matrix products, tn(): lax.dot_general(left, right, (((0,), (0,)), ((), ())), preferred_element_...  16.2 us
    ppermute x11, starting transfers between devices, flipped(): return lax.ppermute(x, 'dp', [(i, i ^ bit) for i in range(rows_dp)])  12.2 us
    ppermute x4, starting transfers between devices, shifted(): return lax.ppermute(x, ('head', 'blk'), pairs)  11.1 us
    unnamed x51, local copies, waits for them, and re-layouts  10.3 us
  transfers between devices with their start and end apart: 25, of which 19 were waited for; matrix products, arithmetic and copies ran while one was open for 7% of the time, Pallas kernels for 0%

profile of v3, /device:TPU:0, one launch (start us, length us, event | category | flops | bytes accessed | tf_op | source)
XLA Modules:
  0.0 331.4 jit_solution(2196907998111335180)
XLA Ops:
  8.2 4.9 %collective-permute-start.1 = (bf16[128,2048]{1,0:T(8,128)(2,1)S(1)}, bf16[128,2048]{1,0:T(8,128)(2,1)S(1)}, u32[]{:S(2)}, u32[]{:S(2)}) collective-permute-start(bf16[128,2048]{1,0:T(8,128)(2,1)S(1)} %pad_maximum_fusion.6), channel_id=1, source_target_pairs={{0,4},{4,1},{1,5},{5,2},{2,6},{6,3},{3,7},{8,12},{12,9},{9,13},{13... | collective-permute-start | bytes 1572872 | tf_op jit(solution)/shard_map/ppermute | solution.py:135
  13.1 3.5 %collective-permute-start = (bf16[128,2048]{1,0:T(8,128)(2,1)S(1)}, bf16[128,2048]{1,0:T(8,128)(2,1)S(1)}, u32[]{:S(2)}, u32[]{:S(2)}) collective-permute-start(bf16[128,2048]{1,0:T(8,128)(2,1)S(1)} %pad_maximum_fusion.6), channel_id=1, source_target_pairs={{0,1},{4,5},{1,2},{5,6},{2,3},{6,7},{8,9},{12,13},{9,10},{13,14},{... | collective-permute-start | bytes 1572872 | tf_op jit(solution)/shard_map/ppermute | solution.py:135
  18.0 3.3 all-to-all-start
  21.3 2.7 multiply_bitcast_fusion
  24.1 2.7 copy.15
  26.8 3.4 %reduce_sum.9 = f32[128,64]{1,0:T(8,128)S(1)} reduce(f32[128,64,128]{2,1,0:T(8,128)} %bitcast.44, f32[]{:T(128)} %constant.58.clone.1), dimensions={2}, to_apply=%region_0.0 | reduce | flops 1040384 | bytes 4227076 | tf_op jit(solution)/shard_map/reduce_sum | solution.py:199
  32.3 1.1 copy-done.1
  33.5 1.6 copy-done.3
  35.1 7.9 %shard_map.111 = (bf16[128,8192]{1,0:T(8,128)(2,1)}, f32[128,1024]{1,0:T(8,128)S(1)}, f32[128,1024]{1,0:T(8,128)S(1)}, bf16[256,1024]{1,0:T(8,128)(2,1)S(1)}, bf16[256,1024]{1,0:T(8,128)(2,1)S(1)}) custom-call(s32[8]{0:T(128)S(1)} %bitcast.43, s32[1]{0:T(128)} %bitcast.1.base_ref, bf16[128,8192]{1,0:T(8,128)(2,1)S(1)} %bitcast.42, ...), custom_call_target="tpu_custom_call" | custom-call | flops 30000001024 | bytes 10000000 | tf_op jit(solution)/shard_map/pallas_call | solution.py:96
  43.9 1.4 collective-permute-start.3
  46.2 1.3 collective-permute-start.2
  47.5 14.4 %collective-permute-done.3 = bf16[128,2048]{1,0:T(8,128)(2,1)S(1)} collective-permute-done((bf16[128,2048]{1,0:T(8,128)(2,1)}, bf16[128,2048]{1,0:T(8,128)(2,1)S(1)}, u32[]{:S(2)}, u32[]{:S(2)}) %collective-permute-start.3) | collective-permute-done | bytes 524320 | tf_op jit(solution)/shard_map/ppermute | solution.py:135
  61.9 8.9 %collective-permute-done.2 = bf16[128,2048]{1,0:T(8,128)(2,1)} collective-permute-done((bf16[128,2048]{1,0:T(8,128)(2,1)}, bf16[128,2048]{1,0:T(8,128)(2,1)}, u32[]{:S(2)}, u32[]{:S(2)}) %collective-permute-start.2) | collective-permute-done | bytes 524320 | tf_op jit(solution)/shard_map/ppermute | solution.py:135
  70.7 2.2 convert_add_fusion
  74.0 4.7 %collective-permute-start.17 = (bf16[128,1024]{1,0:T(8,128)(2,1)S(1)}, bf16[128,1024]{1,0:T(8,128)(2,1)S(1)}, u32[]{:S(2)}, u32[]{:S(2)}) collective-permute-start(bf16[128,1024]{1,0:T(8,128)(2,1)S(1)} %get-tuple-element.32), channel_id=1, source_target_pairs={{0,4},{4,0},{1,5},{5,1},{2,6},{6,2},{3,7},{7,3},{8,12},{12,8},{9,1... | collective-permute-start | bytes 786440 | tf_op jit(solution)/shard_map/ppermute | solution.py:162
  78.7 5.6 %collective-permute-done.17 = bf16[128,1024]{1,0:T(8,128)(2,1)S(1)} collective-permute-done((bf16[128,1024]{1,0:T(8,128)(2,1)S(1)}, bf16[128,1024]{1,0:T(8,128)(2,1)S(1)}, u32[]{:S(2)}, u32[]{:S(2)}) %collective-permute-start.17) | collective-permute-done | bytes 262176 | tf_op jit(solution)/shard_map/ppermute | solution.py:162
  84.3 1.1 collective-permute-start.18
  85.5 11.4 %collective-permute-done.18 = bf16[256,1024]{1,0:T(8,128)(2,1)S(1)} collective-permute-done((bf16[256,1024]{1,0:T(8,128)(2,1)S(1)}, bf16[256,1024]{1,0:T(8,128)(2,1)S(1)}, u32[]{:S(2)}, u32[]{:S(2)}) %collective-permute-start.18) | collective-permute-done | bytes 524320 | tf_op jit(solution)/shard_map/ppermute | solution.py:171
  97.8 2.5 collective-permute-start.19
  100.3 6.5 %collective-permute-done.7 = bf16[128,4096]{1,0:T(8,128)(2,1)S(1)} collective-permute-done((bf16[128,4096]{1,0:T(8,128)(2,1)}, bf16[128,4096]{1,0:T(8,128)(2,1)S(1)}, u32[]{:S(2)}, u32[]{:S(2)}) %collective-permute-start.7) | collective-permute-done | bytes 1048608 | tf_op jit(solution)/shard_map/ppermute | solution.py:162
  106.8 1.4 fusion.45
  108.2 1.4 collective-permute-start.9
  109.7 1.6 collective-permute-start.8
  111.2 9.6 %collective-permute-done.10 = bf16[256,1024]{1,0:T(8,128)(2,1)S(1)} collective-permute-done((bf16[256,1024]{1,0:T(8,128)(2,1)S(1)}, bf16[256,1024]{1,0:T(8,128)(2,1)S(1)}, u32[]{:S(2)}, u32[]{:S(2)}) %collective-permute-start.10) | collective-permute-done | bytes 524320 | tf_op jit(solution)/shard_map/ppermute | solution.py:171
  120.8 12.9 %collective-permute-done.8 = bf16[256,1024]{1,0:T(8,128)(2,1)S(1)} collective-permute-done((bf16[256,1024]{1,0:T(8,128)(2,1)S(1)}, bf16[256,1024]{1,0:T(8,128)(2,1)S(1)}, u32[]{:S(2)}, u32[]{:S(2)}) %collective-permute-start.8) | collective-permute-done | bytes 524320 | tf_op jit(solution)/shard_map/ppermute | solution.py:171
  134.5 5.0 %fusion.32 = bf16[1024,1024]{1,0:T(8,128)(2,1)} fusion(bf16[512,1024]{1,0:T(8,128)(2,1)} %collective-permute-done.19, bf16[256,1024]{1,0:T(8,128)(2,1)S(1)} %copy-done.9, bf16[128,1024]{1,0:T(8,128)(2,1)S(1)} %collective-permute-done.17, bf16[128,1024]{1,0:T(8,128)(2,1)S(1)} %get-tuple-element.33, bf16[256,1024]{1,0:T(8,128)(2,1)S(1)} %collective-permute-done.10, ...), kind=kOutput, calls=%fused_computation.43 | convolution fusion | flops 2165309440 | bytes 6291456 | tf_op jit(solution)/shard_map/dot_general | solution.py:20
  140.4 2.3 collective-permute-start.14
  142.8 5.3 %collective-permute-done.14 = bf16[128,1024]{1,0:T(8,128)(2,1)S(1)} collective-permute-done((bf16[128,1024]{1,0:T(8,128)(2,1)S(1)}, bf16[128,1024]{1,0:T(8,128)(2,1)S(1)}, u32[]{:S(2)}, u32[]{:S(2)}) %collective-permute-start.14) | collective-permute-done | bytes 262176 | tf_op jit(solution)/shard_map/ppermute | solution.py:162
  148.1 1.6 collective-permute-start.15
  149.7 11.7 %collective-permute-done.15 = bf16[256,1024]{1,0:T(8,128)(2,1)S(1)} collective-permute-done((bf16[256,1024]{1,0:T(8,128)(2,1)S(1)}, bf16[256,1024]{1,0:T(8,128)(2,1)S(1)}, u32[]{:S(2)}, u32[]{:S(2)}) %collective-permute-start.15) | collective-permute-done | bytes 524320 | tf_op jit(solution)/shard_map/ppermute | solution.py:171
  161.6 2.6 collective-permute-done.16
  164.3 3.8 %fusion.35 = bf16[1024,1024]{1,0:T(8,128)(2,1)} fusion(bf16[512,1024]{1,0:T(8,128)(2,1)S(1)} %collective-permute-done.16, bf16[256,1024]{1,0:T(8,128)(2,1)S(1)} %collective-permute-done.15, bf16[128,1024]{1,0:T(8,128)(2,1)S(1)} %collective-permute-done.14, bf16[128,1024]{1,0:T(8,128)(2,1)S(1)} %get-tuple-element.28, bf16[256,1024]{1,0:T(8,128)(2,1)S(1)} %copy-done.16, ...), kind=kOutput, calls=%fused_computation.44 | convolution fusion | flops 2165309440 | bytes 6291456 | tf_op jit(solution)/shard_map/dot_general | solution.py:20
  169.0 1.4 collective-permute-start.11
  170.4 6.9 %collective-permute-done.11 = bf16[128,1024]{1,0:T(8,128)(2,1)S(1)} collective-permute-done((bf16[128,1024]{1,0:T(8,128)(2,1)S(1)}, bf16[128,1024]{1,0:T(8,128)(2,1)S(1)}, u32[]{:S(2)}, u32[]{:S(2)}) %collective-permute-start.11) | collective-permute-done | bytes 262176 | tf_op jit(solution)/shard_map/ppermute | solution.py:162
  177.4 1.8 collective-permute-start.12
  179.2 11.5 %collective-permute-done.12 = bf16[256,1024]{1,0:T(8,128)(2,1)S(1)} collective-permute-done((bf16[256,1024]{1,0:T(8,128)(2,1)S(1)}, bf16[256,1024]{1,0:T(8,128)(2,1)S(1)}, u32[]{:S(2)}, u32[]{:S(2)}) %collective-permute-start.12) | collective-permute-done | bytes 524320 | tf_op jit(solution)/shard_map/ppermute | solution.py:171
  190.8 2.6 collective-permute-done.13
  193.5 3.7 %fusion.38 = bf16[1024,1024]{1,0:T(8,128)(2,1)} fusion(bf16[512,1024]{1,0:T(8,128)(2,1)S(1)} %collective-permute-done.13, bf16[256,1024]{1,0:T(8,128)(2,1)S(1)} %collective-permute-done.12, bf16[128,1024]{1,0:T(8,128)(2,1)S(1)} %collective-permute-done.11, bf16[128,1024]{1,0:T(8,128)(2,1)S(1)} %get-tuple-element.30, bf16[256,1024]{1,0:T(8,128)(2,1)S(1)} %copy-done.17, ...), kind=kOutput, calls=%fused_computation.45 | convolution fusion | flops 2165309440 | bytes 6291456 | tf_op jit(solution)/shard_map/dot_general | solution.py:20
  198.1 1.4 collective-permute-start.4
  199.6 6.9 %collective-permute-done.4 = bf16[128,1024]{1,0:T(8,128)(2,1)S(1)} collective-permute-done((bf16[128,1024]{1,0:T(8,128)(2,1)S(1)}, bf16[128,1024]{1,0:T(8,128)(2,1)S(1)}, u32[]{:S(2)}, u32[]{:S(2)}) %collective-permute-start.4) | collective-permute-done | bytes 262176 | tf_op jit(solution)/shard_map/ppermute | solution.py:162
  206.5 1.8 collective-permute-start.5
  208.3 11.5 %collective-permute-done.5 = bf16[256,1024]{1,0:T(8,128)(2,1)S(1)} collective-permute-done((bf16[256,1024]{1,0:T(8,128)(2,1)S(1)}, bf16[256,1024]{1,0:T(8,128)(2,1)S(1)}, u32[]{:S(2)}, u32[]{:S(2)}) %collective-permute-start.5) | collective-permute-done | bytes 524320 | tf_op jit(solution)/shard_map/ppermute | solution.py:171
  220.0 2.6 collective-permute-done.6
  222.6 3.7 %fusion.41 = bf16[1024,1024]{1,0:T(8,128)(2,1)} fusion(bf16[512,1024]{1,0:T(8,128)(2,1)S(1)} %collective-permute-done.6, bf16[256,1024]{1,0:T(8,128)(2,1)S(1)} %collective-permute-done.5, bf16[128,1024]{1,0:T(8,128)(2,1)S(1)} %collective-permute-done.4, bf16[128,1024]{1,0:T(8,128)(2,1)S(1)} %get-tuple-element.26, bf16[256,1024]{1,0:T(8,128)(2,1)S(1)} %copy-done.17, ...), kind=kOutput, calls=%fused_computation.46 | convolution fusion | flops 2165309440 | bytes 6291456 | tf_op jit(solution)/shard_map/dot_general | solution.py:20
  226.4 4.4 %reduce-scatter.9.cloned.1.call-done = bf16[1024,256]{1,0:T(8,128)(2,1)} async-done(((bf16[1024,1024]{1,0:T(8,128)(2,1)}), bf16[1024,256]{1,0:T(8,128)(2,1)}) %reduce-scatter.9.cloned.1.call-update) | async-done | bytes 524304 | tf_op jit(solution)/shard_map/reduce_scatter | solution.py:192
  230.8 45.6 %reduce-scatter.7.cloned.1.call-done = bf16[1024,256]{1,0:T(8,128)(2,1)} async-done(((bf16[1024,1024]{1,0:T(8,128)(2,1)}), bf16[1024,256]{1,0:T(8,128)(2,1)}) %reduce-scatter.7.cloned.1.call-update) | async-done | bytes 524304 | tf_op jit(solution)/shard_map/reduce_scatter | solution.py:192
  276.5 45.5 %reduce-scatter.5.cloned.1.call-done = bf16[1024,256]{1,0:T(8,128)(2,1)} async-done(((bf16[1024,1024]{1,0:T(8,128)(2,1)}), bf16[1024,256]{1,0:T(8,128)(2,1)}) %reduce-scatter.5.cloned.1.call-update) | async-done | bytes 524304 | tf_op jit(solution)/shard_map/reduce_scatter | solution.py:192
  321.9 3.0 pad_maximum_fusion.1
  (85 shorter events, 12.6 us)
Async XLA Ops:
  8.2 22.0 %collective-permute-start.1 = (bf16[128,2048]{1,0:T(8,128)(2,1)S(1)}, bf16[128,2048]{1,0:T(8,128)(2,1)S(1)}, u32[]{:S(2)}, u32[]{:S(2)}) collective-permute-start(bf16[128,2048]{1,0:T(8,128)(2,1)S(1)} %pad_maximum_fusion.6), channel_id=1, source_target_pairs={{0,4},{4,1},{1,5},{5,2},{2,6},{6,3},{3,7},{8,12},{12,9},{9,13},{13... | collective-permute-start | bytes 1572872 | tf_op jit(solution)/shard_map/ppermute | solution.py:135
  13.1 17.1 %collective-permute-start = (bf16[128,2048]{1,0:T(8,128)(2,1)S(1)}, bf16[128,2048]{1,0:T(8,128)(2,1)S(1)}, u32[]{:S(2)}, u32[]{:S(2)}) collective-permute-start(bf16[128,2048]{1,0:T(8,128)(2,1)S(1)} %pad_maximum_fusion.6), channel_id=1, source_target_pairs={{0,1},{4,5},{1,2},{5,6},{2,3},{6,7},{8,9},{12,13},{9,10},{13,14},{... | collective-permute-start | bytes 1572872 | tf_op jit(solution)/shard_map/ppermute | solution.py:135
  18.0 13.5 %all-to-all-start = ((f32[32,2,128]{2,0,1:T(8,128)}), f32[32,2,128]{2,0,1:T(8,128)S(1)}, u32[]{:S(2)}, u32[]{:S(2)}) async-start(f32[32,2,128]{2,0,1:T(8,128)} %copy.13), calls=%async_computation | async-start | bytes 65536 | tf_op jit(solution)/shard_map/all_to_all | solution.py:198
  21.3 205.2 %reduce-scatter.11.cloned.1.call-start = ((), (), s32[]{:S(2)}) async-start(), calls=%async_computation.8 | async-start | bytes 2621440 | tf_op jit(solution)/shard_map/reduce_scatter | solution.py:192
  26.8 3.5 %copy-start.6 = (bf16[1,128,1024]{2,1,0:T(8,128)(2,1)S(1)}, bf16[1,128,1024]{2,1,0:T(8,128)(2,1)}, u32[]{:S(2)}) copy-start(bf16[1,128,1024]{2,1,0:T(8,128)(2,1)} %param.10) | copy-start | bytes 786436
  26.8 3.5 %copy-start.7 = (bf16[1,128,1024]{2,1,0:T(8,128)(2,1)S(1)}, bf16[1,128,1024]{2,1,0:T(8,128)(2,1)}, u32[]{:S(2)}) copy-start(bf16[1,128,1024]{2,1,0:T(8,128)(2,1)} %param.9) | copy-start | bytes 786436
  30.4 1.9 copy-start
  30.5 1.9 copy-start.4
  32.3 1.1 copy-start.1
  33.5 1.6 copy-start.3
  43.0 3.3 copy-start.2
  43.9 29.0 %copy-start.5 = (bf16[1,128,8192]{2,1,0:T(8,128)(2,1)S(1)}, bf16[1,128,8192]{2,1,0:T(8,128)(2,1)}, u32[]{:S(2)}) copy-start(bf16[1,128,8192]{2,1,0:T(8,128)(2,1)} %param.11) | copy-start | bytes 6291460
  43.9 18.0 %collective-permute-start.3 = (bf16[128,2048]{1,0:T(8,128)(2,1)}, bf16[128,2048]{1,0:T(8,128)(2,1)S(1)}, u32[]{:S(2)}, u32[]{:S(2)}) collective-permute-start(bf16[128,2048]{1,0:T(8,128)(2,1)} %pad_maximum_fusion.8), channel_id=1, source_target_pairs={{1,0},{5,4},{2,1},{6,5},{3,2},{7,6},{9,8},{13,12},{10,9},{14,13},{... | collective-permute-start | bytes 1572872 | tf_op jit(solution)/shard_map/ppermute | solution.py:135
  46.2 24.5 %collective-permute-start.2 = (bf16[128,2048]{1,0:T(8,128)(2,1)}, bf16[128,2048]{1,0:T(8,128)(2,1)}, u32[]{:S(2)}, u32[]{:S(2)}) collective-permute-start(bf16[128,2048]{1,0:T(8,128)(2,1)} %pad_maximum_fusion.7), channel_id=1, source_target_pairs={{4,0},{1,4},{5,1},{2,5},{6,2},{3,6},{7,3},{12,8},{9,12},{13,9},{10... | collective-permute-start | bytes 1572872 | tf_op jit(solution)/shard_map/ppermute | solution.py:135
  74.0 10.3 %collective-permute-start.17 = (bf16[128,1024]{1,0:T(8,128)(2,1)S(1)}, bf16[128,1024]{1,0:T(8,128)(2,1)S(1)}, u32[]{:S(2)}, u32[]{:S(2)}) collective-permute-start(bf16[128,1024]{1,0:T(8,128)(2,1)S(1)} %get-tuple-element.32), channel_id=1, source_target_pairs={{0,4},{4,0},{1,5},{5,1},{2,6},{6,2},{3,7},{7,3},{8,12},{12,8},{9,1... | collective-permute-start | bytes 786440 | tf_op jit(solution)/shard_map/ppermute | solution.py:162
  78.7 28.1 %collective-permute-start.7 = (bf16[128,4096]{1,0:T(8,128)(2,1)}, bf16[128,4096]{1,0:T(8,128)(2,1)S(1)}, u32[]{:S(2)}, u32[]{:S(2)}) collective-permute-start(bf16[128,4096]{1,0:T(8,128)(2,1)} %bitcast.15), channel_id=1, source_target_pairs={{0,4},{4,0},{1,5},{5,1},{2,6},{6,2},{3,7},{7,3},{8,12},{12,8},{9,1... | collective-permute-start | bytes 3145736 | tf_op jit(solution)/shard_map/ppermute | solution.py:162
  84.3 12.5 %collective-permute-start.18 = (bf16[256,1024]{1,0:T(8,128)(2,1)S(1)}, bf16[256,1024]{1,0:T(8,128)(2,1)S(1)}, u32[]{:S(2)}, u32[]{:S(2)}) collective-permute-start(bf16[256,1024]{1,0:T(8,128)(2,1)S(1)} %pad_maximum_fusion.12), channel_id=1, source_target_pairs={{0,16},{8,24},{16,0},{24,8},{1,17},{9,25},{17,1},{25,9},{2,18},{10... | collective-permute-start | bytes 1572872 | tf_op jit(solution)/shard_map/ppermute | solution.py:171
  97.8 35.9 %collective-permute-start.19 = (bf16[512,1024]{1,0:T(8,128)(2,1)S(1)}, bf16[512,1024]{1,0:T(8,128)(2,1)}, u32[]{:S(2)}, u32[]{:S(2)}) collective-permute-start(bf16[512,1024]{1,0:T(8,128)(2,1)S(1)} %pad_maximum_fusion.5), channel_id=1, source_target_pairs={{0,8},{8,0},{16,24},{24,16},{1,9},{9,1},{17,25},{25,17},{2,10},{10... | collective-permute-start | bytes 3145736 | tf_op jit(solution)/shard_map/ppermute | solution.py:171
  100.3 34.2 %copy-start.9 = (bf16[256,1024]{1,0:T(8,128)(2,1)S(1)}, bf16[256,1024]{1,0:T(8,128)(2,1)}, u32[]{:S(2)}) copy-start(bf16[256,1024]{1,0:T(8,128)(2,1)} %copy-done.8) | copy-start | bytes 1572868
  108.1 25.5 %copy-start.10 = (bf16[256,1024]{1,0:T(8,128)(2,1)}, bf16[256,1024]{1,0:T(8,128)(2,1)S(1)}, u32[]{:S(2)}) copy-start(bf16[256,1024]{1,0:T(8,128)(2,1)S(1)} %get-tuple-element.34) | copy-start | bytes 1572868
  108.2 12.7 %collective-permute-start.10 = (bf16[256,1024]{1,0:T(8,128)(2,1)S(1)}, bf16[256,1024]{1,0:T(8,128)(2,1)S(1)}, u32[]{:S(2)}, u32[]{:S(2)}) collective-permute-start(bf16[256,1024]{1,0:T(8,128)(2,1)S(1)} %get-tuple-element.37), channel_id=1, source_target_pairs={{0,24},{8,16},{16,8},{24,0},{1,25},{9,17},{17,9},{25,1},{2,26},{10... | collective-permute-start | bytes 1572872 | tf_op jit(solution)/shard_map/ppermute | solution.py:171
  108.2 12.6 %collective-permute-start.9 = (bf16[256,1024]{1,0:T(8,128)(2,1)S(1)}, bf16[256,1024]{1,0:T(8,128)(2,1)S(1)}, u32[]{:S(2)}, u32[]{:S(2)}) collective-permute-start(bf16[256,1024]{1,0:T(8,128)(2,1)S(1)} %get-tuple-element.36), channel_id=1, source_target_pairs={{0,8},{8,0},{16,24},{24,16},{1,9},{9,1},{17,25},{25,17},{2,10},{10... | collective-permute-start | bytes 1572872 | tf_op jit(solution)/shard_map/ppermute | solution.py:171
  109.7 24.0 %collective-permute-start.8 = (bf16[256,1024]{1,0:T(8,128)(2,1)S(1)}, bf16[256,1024]{1,0:T(8,128)(2,1)S(1)}, u32[]{:S(2)}, u32[]{:S(2)}) collective-permute-start(bf16[256,1024]{1,0:T(8,128)(2,1)S(1)} %get-tuple-element.35), channel_id=1, source_target_pairs={{0,16},{8,24},{16,0},{24,8},{1,17},{9,25},{17,1},{25,9},{2,18},{10... | collective-permute-start | bytes 1572872 | tf_op jit(solution)/shard_map/ppermute | solution.py:171
  120.8 12.9 %copy-start.15 = (bf16[256,1024]{1,0:T(8,128)(2,1)}, bf16[256,1024]{1,0:T(8,128)(2,1)S(1)}, u32[]{:S(2)}) copy-start(bf16[256,1024]{1,0:T(8,128)(2,1)S(1)} %collective-permute-done.10) | copy-start | bytes 1572868
  120.8 18.6 %copy-start.18 = (bf16[256,1024]{1,0:T(8,128)(2,1)}, bf16[256,1024]{1,0:T(8,128)(2,1)S(1)}, u32[]{:S(2)}) copy-start(bf16[256,1024]{1,0:T(8,128)(2,1)S(1)} %collective-permute-done.9) | copy-start | bytes 1572868
  139.5 1.0 copy-start.14
  139.5 24.8 %copy-start.11 = (bf16[256,1024]{1,0:T(8,128)(2,1)S(1)}, bf16[256,1024]{1,0:T(8,128)(2,1)}, u32[]{:S(2)}) copy-start(bf16[256,1024]{1,0:T(8,128)(2,1)} %copy-done.10) | copy-start | bytes 1572868
  139.5 91.3 %reduce-scatter.9.cloned.1.call-start = ((), (), s32[]{:S(2)}) async-start(), calls=%async_computation.7 | async-start | bytes 2621440 | tf_op jit(solution)/shard_map/reduce_scatter | solution.py:192
  139.5 24.7 %copy-start.16 = (bf16[256,1024]{1,0:T(8,128)(2,1)S(1)}, bf16[256,1024]{1,0:T(8,128)(2,1)}, u32[]{:S(2)}) copy-start(bf16[256,1024]{1,0:T(8,128)(2,1)} %copy-done.15) | copy-start | bytes 1572868
  139.5 24.7 %copy-start.19 = (bf16[256,1024]{1,0:T(8,128)(2,1)S(1)}, bf16[256,1024]{1,0:T(8,128)(2,1)}, u32[]{:S(2)}) copy-start(bf16[256,1024]{1,0:T(8,128)(2,1)} %copy-done.18) | copy-start | bytes 1572868
  139.6 24.7 %copy-start.22 = (bf16[256,1024]{1,0:T(8,128)(2,1)S(1)}, bf16[256,1024]{1,0:T(8,128)(2,1)}, u32[]{:S(2)}) copy-start(bf16[256,1024]{1,0:T(8,128)(2,1)} %copy-done.21) | copy-start | bytes 1572868
  140.4 7.7 %collective-permute-start.14 = (bf16[128,1024]{1,0:T(8,128)(2,1)S(1)}, bf16[128,1024]{1,0:T(8,128)(2,1)S(1)}, u32[]{:S(2)}, u32[]{:S(2)}) collective-permute-start(bf16[128,1024]{1,0:T(8,128)(2,1)S(1)} %copy-done.14), channel_id=1, source_target_pairs={{0,4},{4,0},{1,5},{5,1},{2,6},{6,2},{3,7},{7,3},{8,12},{12,8},{9,1... | collective-permute-start | bytes 786440 | tf_op jit(solution)/shard_map/ppermute | solution.py:162
  148.1 13.3 %collective-permute-start.15 = (bf16[256,1024]{1,0:T(8,128)(2,1)S(1)}, bf16[256,1024]{1,0:T(8,128)(2,1)S(1)}, u32[]{:S(2)}, u32[]{:S(2)}) collective-permute-start(bf16[256,1024]{1,0:T(8,128)(2,1)S(1)} %pad_maximum_fusion.11), channel_id=1, source_target_pairs={{0,16},{8,24},{16,0},{24,8},{1,17},{9,25},{17,1},{25,9},{2,18},{10... | collective-permute-start | bytes 1572872 | tf_op jit(solution)/shard_map/ppermute | solution.py:171
  161.5 2.7 collective-permute-start.16
  168.0 1.0 copy-start.13
  168.1 25.4 %copy-start.17 = (bf16[256,1024]{1,0:T(8,128)(2,1)S(1)}, bf16[256,1024]{1,0:T(8,128)(2,1)}, u32[]{:S(2)}) copy-start(bf16[256,1024]{1,0:T(8,128)(2,1)} %copy-done.15) | copy-start | bytes 1572868
  168.1 25.4 %copy-start.20 = (bf16[256,1024]{1,0:T(8,128)(2,1)S(1)}, bf16[256,1024]{1,0:T(8,128)(2,1)}, u32[]{:S(2)}) copy-start(bf16[256,1024]{1,0:T(8,128)(2,1)} %copy-done.18) | copy-start | bytes 1572868
  168.1 108.4 %reduce-scatter.7.cloned.1.call-start = ((), (), s32[]{:S(2)}) async-start(), calls=%async_computation.6 | async-start | bytes 2621440 | tf_op jit(solution)/shard_map/reduce_scatter | solution.py:192
  168.3 25.2 %copy-start.23 = (bf16[256,1024]{1,0:T(8,128)(2,1)S(1)}, bf16[256,1024]{1,0:T(8,128)(2,1)}, u32[]{:S(2)}) copy-start(bf16[256,1024]{1,0:T(8,128)(2,1)} %copy-done.21) | copy-start | bytes 1572868
  169.0 8.3 %collective-permute-start.11 = (bf16[128,1024]{1,0:T(8,128)(2,1)S(1)}, bf16[128,1024]{1,0:T(8,128)(2,1)S(1)}, u32[]{:S(2)}, u32[]{:S(2)}) collective-permute-start(bf16[128,1024]{1,0:T(8,128)(2,1)S(1)} %copy-done.13), channel_id=1, source_target_pairs={{0,4},{4,0},{1,5},{5,1},{2,6},{6,2},{3,7},{7,3},{8,12},{12,8},{9,1... | collective-permute-start | bytes 786440 | tf_op jit(solution)/shard_map/ppermute | solution.py:162
  177.4 13.3 %collective-permute-start.12 = (bf16[256,1024]{1,0:T(8,128)(2,1)S(1)}, bf16[256,1024]{1,0:T(8,128)(2,1)S(1)}, u32[]{:S(2)}, u32[]{:S(2)}) collective-permute-start(bf16[256,1024]{1,0:T(8,128)(2,1)S(1)} %pad_maximum_fusion.10), channel_id=1, source_target_pairs={{0,16},{8,24},{16,0},{24,8},{1,17},{9,25},{17,1},{25,9},{2,18},{10... | collective-permute-start | bytes 1572872 | tf_op jit(solution)/shard_map/ppermute | solution.py:171
  190.7 2.7 collective-permute-start.13
  197.2 0.9 copy-start.12
  197.2 124.7 %reduce-scatter.5.cloned.1.call-start = ((), (), s32[]{:S(2)}) async-start(), calls=%async_computation.5 | async-start | bytes 2621440 | tf_op jit(solution)/shard_map/reduce_scatter | solution.py:192
  197.3 25.4 %copy-start.24 = (bf16[256,1024]{1,0:T(8,128)(2,1)S(1)}, bf16[256,1024]{1,0:T(8,128)(2,1)}, u32[]{:S(2)}) copy-start(bf16[256,1024]{1,0:T(8,128)(2,1)} %copy-done.21) | copy-start | bytes 1572868
  198.1 8.3 %collective-permute-start.4 = (bf16[128,1024]{1,0:T(8,128)(2,1)S(1)}, bf16[128,1024]{1,0:T(8,128)(2,1)S(1)}, u32[]{:S(2)}, u32[]{:S(2)}) collective-permute-start(bf16[128,1024]{1,0:T(8,128)(2,1)S(1)} %copy-done.12), channel_id=1, source_target_pairs={{0,4},{4,0},{1,5},{5,1},{2,6},{6,2},{3,7},{7,3},{8,12},{12,8},{9,1... | collective-permute-start | bytes 786440 | tf_op jit(solution)/shard_map/ppermute | solution.py:162
  206.5 13.3 %collective-permute-start.5 = (bf16[256,1024]{1,0:T(8,128)(2,1)S(1)}, bf16[256,1024]{1,0:T(8,128)(2,1)S(1)}, u32[]{:S(2)}, u32[]{:S(2)}) collective-permute-start(bf16[256,1024]{1,0:T(8,128)(2,1)S(1)} %pad_maximum_fusion.9), channel_id=1, source_target_pairs={{0,16},{8,24},{16,0},{24,8},{1,17},{9,25},{17,1},{25,9},{2,18},{10... | collective-permute-start | bytes 1572872 | tf_op jit(solution)/shard_map/ppermute | solution.py:171
  219.9 2.7 collective-permute-start.6
  (2 other events, 1.6 us)
Sparse Core Ops, SparseCore 0:
  139.6 45.6 reduce-scatter.10
  187.7 43.0 reduce-scatter.8
  233.1 43.2 reduce-scatter.6
  278.7 43.1 reduce-scatter.4
